TPU v7x, 512 devices: a whole 4x4x16 slice. The times are simulated.
512 devices in a mesh: seq: 128 (over x, z, core), head: 4 (over y).
Axes of the slice: x: 4, y: 4, z: 16, core: 2. Of those that a mesh axis runs over, the one named last changes fastest.
Arguments:
- queries: bfloat16 [32768, 1024], P('seq', 'head'), may hold values from -8 to 8
- keys: bfloat16 [32768, 1024], P('seq', 'head'), may hold values from -8 to 8
- values: bfloat16 [32768, 1024], P('seq', 'head'), may hold values from -6 to 6
- out_grad: bfloat16 [32768, 1024], P('seq', 'head'), may hold values from -6 to 6
- w_out: bfloat16 [1024, 1024], P('head'), may hold values from -0.1875 to 0.1875
- cluster_ids: int32 [16, 32768, 1], P('head', 'seq'), may hold values from 0 to 255; in each aligned block of 256 rows (0 to 255, 256 to 511, ..., all dimensions but the last counted through in order) at most 2 rows name the same one
Outputs:
- query_grad: bfloat16 [32768, 1024], P('seq', 'head')
- key_grad: bfloat16 [32768, 1024], P('seq', 'head')
- value_grad: bfloat16 [32768, 1024], P('seq', 'head')
- centroid_sums: float32 [256, 1024], P('seq', 'head')
Inputs may be any that keep to these rules, and one draw needn't show every extreme that they name: `cluster_ids`: within each head, among the frames of one device, no cluster is named by more than 2 frames.
All inputs are finite; a program needn't handle non-finite values.
Results may differ from a plain program's by a relative error of at most 0.012.
The roundings to bfloat16 on the way count: a program that leaves them out, or rounds other values in their place, can miss the bound.
Values may be sent and summed in bfloat16 or wider, within the bound.
A program may use at most 64 MiB of HBM per device.

v0:
```python
import jax
import jax.numpy as jnp
from jax import lax
from jax.sharding import PartitionSpec as P

HD = 64
CLUSTERS = 256
MOST = 2


def cluster_block(block, live):
    q_rows = block[:, :HD]
    k_rows = block[:, HD : 2 * HD]
    v_rows = block[:, 2 * HD : 3 * HD]
    g_rows = block[:, 3 * HD :]
    scores = 0.125 * jnp.dot(q_rows, k_rows.T, preferred_element_type=jnp.float32)
    scores = jnp.where(live[None, :], scores, jnp.float32(-1e30))
    top = jnp.max(scores, axis=1, keepdims=True)
    expo = jnp.exp(scores - top)
    probs = expo / jnp.sum(expo, axis=1, keepdims=True)
    probs_low = probs.astype(jnp.bfloat16)
    attended = jnp.dot(probs_low, v_rows, preferred_element_type=jnp.float32)
    delta = jnp.sum(g_rows.astype(jnp.float32) * attended, axis=1, keepdims=True)
    dprobs = jnp.dot(g_rows, v_rows.T, preferred_element_type=jnp.float32)
    dscores = (probs * (dprobs - delta)).astype(jnp.bfloat16)
    dq_rows = (0.125 * jnp.dot(dscores, k_rows, preferred_element_type=jnp.float32)).astype(
        jnp.bfloat16
    )
    dk_rows = (0.125 * jnp.dot(dscores.T, q_rows, preferred_element_type=jnp.float32)).astype(
        jnp.bfloat16
    )
    dv_rows = jnp.dot(probs_low.T, g_rows, preferred_element_type=jnp.float32).astype(jnp.bfloat16)
    return jnp.concatenate([dq_rows, dk_rows, dv_rows], axis=1)


def attend(received, got_counts):
    count_items = received.shape[0]
    owners = received.shape[1]
    per_owner = got_counts.shape[2]
    capacity = owners * MOST
    blocks = received.reshape(count_items, owners, per_owner, MOST, 4 * HD)
    blocks = blocks.transpose(0, 2, 1, 3, 4).reshape(count_items * per_owner, capacity, 4 * HD)
    live = (
        jnp.arange(MOST, dtype=jnp.int32)[None, None, None, :]
        < got_counts.astype(jnp.int32)[:, :, :, None]
    )
    live = live.transpose(0, 2, 1, 3).reshape(count_items * per_owner, capacity)
    grads = lax.map(lambda pair: cluster_block(pair[0], pair[1]), (blocks, live))
    grads = grads.reshape(count_items, per_owner, owners, MOST, 3 * HD).transpose(0, 2, 1, 3, 4)
    returned = grads.reshape(count_items, owners, per_owner * MOST, 3 * HD)
    key_sums = jnp.sum(blocks[:, :, HD : 2 * HD].astype(jnp.float32), axis=1).reshape(
        count_items, per_owner, HD
    )
    return (returned, key_sums)


def shards(queries, keys, values, out_grad, w_out, cluster_ids):
    frames = queries.shape[0]
    heads = cluster_ids.shape[0]
    owners = lax.axis_size("seq")
    per_owner = CLUSTERS // owners
    d_out = lax.dot_general(
        lax.all_gather(out_grad, "head", axis=1, tiled=True),
        w_out,
        (((1,), (1,)), ((), ())),
        preferred_element_type=jnp.float32,
    ).astype(jnp.bfloat16)

    def split_heads(array):
        return array.reshape(frames, heads, HD).transpose(1, 0, 2)

    key_heads = split_heads(keys)
    rows = jnp.concatenate(
        [split_heads(queries), key_heads, split_heads(values), split_heads(d_out)], axis=2
    )
    ids = cluster_ids[:, :, 0]
    member = (ids[:, :, None] == jnp.arange(CLUSTERS, dtype=jnp.int32)[None, None, :]).astype(
        jnp.int32
    )
    running = jnp.cumsum(member, axis=1)
    rank = jnp.sum(member * (running - 1), axis=2)
    slot = ids * MOST + rank
    counts = running[:, -1, :]
    flat_index = (jnp.arange(heads, dtype=jnp.int32)[:, None] * (CLUSTERS * MOST) + slot).reshape(
        -1
    )
    outgoing = (
        jnp.zeros((heads * CLUSTERS * MOST, 4 * HD), jnp.bfloat16)
        .at[flat_index]
        .set(rows.reshape(-1, 4 * HD))
    )
    outgoing = outgoing.reshape(heads, owners, per_owner * MOST, 4 * HD)
    sent_counts = counts.reshape(heads, owners, per_owner).astype(jnp.bfloat16)
    received, got_counts = (
        lax.all_to_all(outgoing, "seq", split_axis=1, concat_axis=1, tiled=True),
        lax.all_to_all(sent_counts, "seq", split_axis=1, concat_axis=1, tiled=True),
    )
    returned, key_sums = attend(received, got_counts)
    arrived = lax.all_to_all(returned, "seq", split_axis=1, concat_axis=1, tiled=True)
    picked = arrived.reshape(heads * CLUSTERS * MOST, 3 * HD)[flat_index].reshape(
        heads, frames, 3 * HD
    )

    def join_heads(part):
        return part.transpose(1, 0, 2).reshape(frames, heads * HD)

    query_grad = join_heads(picked[:, :, :HD])
    key_grad = join_heads(picked[:, :, HD : 2 * HD])
    value_grad = join_heads(picked[:, :, 2 * HD :])
    member_low = member.astype(jnp.bfloat16)
    local_sums = jnp.einsum(
        "htc,htd->chd", member_low, key_heads, preferred_element_type=jnp.float32
    )
    centroid_sums = lax.psum_scatter(
        local_sums.reshape(CLUSTERS, heads * HD), "seq", scatter_dimension=0, tiled=True
    )
    return (query_grad, key_grad, value_grad, centroid_sums)


def solution(mesh):
    placed = (
        P("seq", "head"),
        P("seq", "head"),
        P("seq", "head"),
        P("seq", "head"),
        P("head", None),
        P("head", "seq", None),
    )
    return jax.shard_map(
        shards,
        mesh=mesh,
        in_specs=placed,
        out_specs=(P("seq", "head"), P("seq", "head"), P("seq", "head"), P("seq", "head")),
        check_vma=False,
    )
```

profile of v0, /device:TPU:1, one launch (start us, length us, event | category | flops | bytes accessed | tf_op | source)
XLA Modules:
  0.0 507.4 jit_solution(4577370519351508553)
XLA Ops:
  7.2 0.9 copy.66
  8.1 0.9 fusion.18
  9.0 0.7 add_add_fusion
  9.8 0.8 copy.68
  10.5 20.5 %all-to-all-start = ((bf16[4,128,2]{0,2,1:T(2,128)(2,1)}), bf16[4,128,2]{0,2,1:T(2,128)(2,1)S(1)}, u32[]{:S(2)}, u32[]{:S(2)}) async-start(bf16[4,128,2]{0,2,1:T(2,128)(2,1)} %bitcast.6), calls=%async_computation | async-start | bytes 131072 | tf_op jit(solution)/shard_map/all_to_all | solution.py:96
  31.7 0.4 copy-done.4
  32.2 0.8 copy-done.3
  33.0 12.2 %all_gather.3 = bf16[256,1024]{1,0:T(8,128)(2,1)S(1)} all-gather(bf16[256,256]{1,0:T(8,128)(2,1)S(1)} %copy-done.3), channel_id=1, replica_groups=mesh['seq'=128,'head'=4] {'head'}, dimensions={1}, use_global_device_ids=true | all-gather | bytes 655360 | tf_op jit(solution)/shard_map/all_gather | solution.py:63
  45.3 0.8 copy-done.6
  46.8 5.3 %scatter_custom_fusion = bf16[2048,256]{1,0:T(8,128)(2,1)S(1)} fusion(s32[1024]{0:T(1024)S(1)} %bitcast.112, bf16[1024,256]{1,0:T(8,128)(2,1)S(1)} %bitcast.101, bf16[]{:T(256)} %constant.10.clone.1), kind=kCustom, calls=%fused_computation.43 | custom fusion | bytes 1048578 | tf_op jit(solution)/shard_map/scatter | solution.py:90
  52.4 1.4 copy.75
  53.8 0.6 copy-done.1
  54.4 17.4 %all-to-all-start.1 = ((bf16[4,128,4,256]{3,2,0,1:T(4,128)(2,1)}), bf16[4,128,4,256]{3,2,0,1:T(4,128)(2,1)S(1)}, u32[]{:S(2)}, u32[]{:S(2)}) async-start(bf16[4,128,4,256]{3,2,0,1:T(4,128)(2,1)} %copy.75), calls=%async_computation.1 | async-start | bytes 2097152 | tf_op jit(solution)/shard_map/all_to_all | solution.py:95
  72.0 0.7 copy-done.2
  73.3 52.9 %all-to-all-done.1 = bf16[4,128,4,256]{3,2,0,1:T(4,128)(2,1)S(1)} async-done(((bf16[4,128,4,256]{3,2,0,1:T(4,128)(2,1)}), bf16[4,128,4,256]{3,2,0,1:T(4,128)(2,1)S(1)}, u32[]{:S(2)}, u32[]{:S(2)}) %all-to-all-start.1) | async-done | bytes 1048608 | tf_op jit(solution)/shard_map/all_to_all | solution.py:95
  126.5 1.1 copy.77
  127.6 0.4 reshape.133
  128.1 12.2 %while.10 = (s32[]{:T(128)}, bf16[8,256,192]{1,2,0:T(8,128)(2,1)S(1)}, pred[8,256]{1,0:T(8,128)(4,1)S(1)}, bf16[8,256,256]{2,1,0:T(8,128)(2,1)S(1)}, s32[]{:T(128)}) while((s32[]{:T(128)}, bf16[8,256,192]{1,2,0:T(8,128)(2,1)S(1)}, pred[8,256]{1,0:T(8,128)(4,1)S(1)}, bf16[8,256,256]{2,1,0:T(8,128)(2,1)S(1)}, s32[]{:T(128)}) %tuple.34), condition=%wide.region_8.9_spmd, body=%wide.region_4.8_spmd.sunk | while | flops 51608832 | bytes 2959433 | solution.py:48
  140.3 0.5 copy.79
  140.8 0.6 reshape.134
  141.4 0.8 copy.80
  142.2 1.7 copy.81
  143.9 8.5 %all-to-all-start.2 = ((bf16[4,128,4,192]{3,2,0,1:T(4,128)(2,1)}), bf16[4,128,4,192]{3,2,0,1:T(4,128)(2,1)S(1)}, u32[]{:S(2)}, u32[]{:S(2)}) async-start(bf16[4,128,4,192]{3,2,0,1:T(4,128)(2,1)} %copy.81), calls=%async_computation.2 | async-start | bytes 2097152 | tf_op jit(solution)/shard_map/all_to_all | solution.py:99
  152.8 0.9 copy.86
  153.7 1.3 dynamic-slice
  155.6 335.7 %all-reduce.3.cloned.1.call-done = f32[256,256]{1,0:T(8,128)} async-done(((f32[256,256]{1,0:T(8,128)}), f32[256,256]{1,0:T(8,128)}) %all-reduce.3.cloned.1.call-update) | async-done | bytes 262160
  491.4 1.3 constant_dynamic-slice_fusion.1
  493.0 0.7 reshape.136
  493.7 3.9 gather_fusion
  498.0 0.8 copy.87
  498.9 0.8 copy.88
  499.8 0.8 copy.89
  (148 shorter events, 16.1 us)
Async XLA Ops:
  7.2 39.0 %copy-start = (bf16[256,1024]{1,0:T(8,128)(2,1)S(1)}, bf16[256,1024]{1,0:T(8,128)(2,1)}, u32[]{:S(2)}) copy-start(bf16[256,1024]{1,0:T(8,128)(2,1)} %param.12) | copy-start | bytes 1572868
  10.5 20.5 %copy-start.7 = (s32[4,256,1]{1,2,0:T(1,128)S(1)}, s32[4,256,1]{1,2,0:T(1,128)}, u32[]{:S(2)}) copy-start(s32[4,256,1]{1,2,0:T(1,128)} %param.13) | copy-start | bytes 12292
  10.5 43.2 %all-to-all-start = ((bf16[4,128,2]{0,2,1:T(2,128)(2,1)}), bf16[4,128,2]{0,2,1:T(2,128)(2,1)S(1)}, u32[]{:S(2)}, u32[]{:S(2)}) async-start(bf16[4,128,2]{0,2,1:T(2,128)(2,1)} %bitcast.6), calls=%async_computation | async-start | bytes 131072 | tf_op jit(solution)/shard_map/all_to_all | solution.py:96
  31.2 0.9 copy-start.4
  32.1 0.9 copy-start.3
  33.0 12.2 %copy-start.5 = (bf16[256,256]{1,0:T(8,128)(2,1)S(1)}, bf16[256,256]{1,0:T(8,128)(2,1)}, u32[]{:S(2)}) copy-start(bf16[256,256]{1,0:T(8,128)(2,1)} %param.8) | copy-start | bytes 393220
  45.2 0.9 copy-start.6
  53.8 0.6 copy-start.1
  54.4 71.8 %all-to-all-start.1 = ((bf16[4,128,4,256]{3,2,0,1:T(4,128)(2,1)}), bf16[4,128,4,256]{3,2,0,1:T(4,128)(2,1)S(1)}, u32[]{:S(2)}, u32[]{:S(2)}) async-start(bf16[4,128,4,256]{3,2,0,1:T(4,128)(2,1)} %copy.75), calls=%async_computation.1 | async-start | bytes 2097152 | tf_op jit(solution)/shard_map/all_to_all | solution.py:95
  71.9 0.8 copy-start.2
  143.9 348.7 %all-to-all-start.2 = ((bf16[4,128,4,192]{3,2,0,1:T(4,128)(2,1)}), bf16[4,128,4,192]{3,2,0,1:T(4,128)(2,1)S(1)}, u32[]{:S(2)}, u32[]{:S(2)}) async-start(bf16[4,128,4,192]{3,2,0,1:T(4,128)(2,1)} %copy.81), calls=%async_computation.2 | async-start | bytes 2097152 | tf_op jit(solution)/shard_map/all_to_all | solution.py:99
  152.4 339.0 %all-reduce.3.cloned.1.call-start = ((), (), s32[]{:S(2)}) async-start(), calls=%async_computation.3 | async-start | bytes 524288
Sparse Core Ops, SparseCore 0:
  156.7 334.6 all-reduce.2
where the time goes:
time: 508 us; the launch traced here: 507 us
  waiting for transfers between devices  389 us (77%)
  starting transfers between devices  46.5 us (9%)
  local copies, waits for them, and re-layouts  31.2 us (6%)
  between operations  15 us (3%)
  blocking collectives  12.2 us (2%)
  matrix products  9.98 us (2%)
    unnamed x2, waiting for transfers between devices  336 us
    all_to_all x1, waiting for transfers between devices, shards(): lax.all_to_all(outgoing, 'seq', split_axis=1, concat_axis=1, tiled=True)  52.9 us
    all_to_all x1, starting transfers between devices, shards(): lax.all_to_all(sent_counts, 'seq', split_axis=1, concat_axis=1, tiled=True)  20.5 us
    all_to_all x1, starting transfers between devices, shards(): lax.all_to_all(outgoing, 'seq', split_axis=1, concat_axis=1, tiled=True)  17.4 us
    all_gather x1, blocking collectives, shards(): lax.all_gather(out_grad, 'head', axis=1, tiled=True)  12.2 us
  transfers between devices with their start and end apart: 4, of which 2 were waited for; matrix products, arithmetic and copies ran while one was open for 3% of the time, Pallas kernels for 0%

commit v1 on v0

--- a/solution.py
+++ b/solution.py
@@ -6,6 +6,7 @@
 HD = 64
 CLUSTERS = 256
 MOST = 2
+EMPTY = 64.0
 
 
 def cluster_block(block, live):
@@ -33,18 +34,13 @@
     return jnp.concatenate([dq_rows, dk_rows, dv_rows], axis=1)
 
 
-def attend(received, got_counts):
+def attend(received, per_owner):
     count_items = received.shape[0]
     owners = received.shape[1]
-    per_owner = got_counts.shape[2]
     capacity = owners * MOST
     blocks = received.reshape(count_items, owners, per_owner, MOST, 4 * HD)
     blocks = blocks.transpose(0, 2, 1, 3, 4).reshape(count_items * per_owner, capacity, 4 * HD)
-    live = (
-        jnp.arange(MOST, dtype=jnp.int32)[None, None, None, :]
-        < got_counts.astype(jnp.int32)[:, :, :, None]
-    )
-    live = live.transpose(0, 2, 1, 3).reshape(count_items * per_owner, capacity)
+    live = blocks[:, :, 0] < EMPTY / 2
     grads = lax.map(lambda pair: cluster_block(pair[0], pair[1]), (blocks, live))
     grads = grads.reshape(count_items, per_owner, owners, MOST, 3 * HD).transpose(0, 2, 1, 3, 4)
     returned = grads.reshape(count_items, owners, per_owner * MOST, 3 * HD)
@@ -80,22 +76,18 @@
     running = jnp.cumsum(member, axis=1)
     rank = jnp.sum(member * (running - 1), axis=2)
     slot = ids * MOST + rank
-    counts = running[:, -1, :]
     flat_index = (jnp.arange(heads, dtype=jnp.int32)[:, None] * (CLUSTERS * MOST) + slot).reshape(
         -1
     )
+    empty_row = jnp.where(jnp.arange(4 * HD) == 0, EMPTY, 0.0).astype(jnp.bfloat16)
     outgoing = (
-        jnp.zeros((heads * CLUSTERS * MOST, 4 * HD), jnp.bfloat16)
+        jnp.broadcast_to(empty_row, (heads * CLUSTERS * MOST, 4 * HD))
         .at[flat_index]
         .set(rows.reshape(-1, 4 * HD))
     )
     outgoing = outgoing.reshape(heads, owners, per_owner * MOST, 4 * HD)
-    sent_counts = counts.reshape(heads, owners, per_owner).astype(jnp.bfloat16)
-    received, got_counts = (
-        lax.all_to_all(outgoing, "seq", split_axis=1, concat_axis=1, tiled=True),
-        lax.all_to_all(sent_counts, "seq", split_axis=1, concat_axis=1, tiled=True),
-    )
-    returned, key_sums = attend(received, got_counts)
+    received = lax.all_to_all(outgoing, "seq", split_axis=1, concat_axis=1, tiled=True)
+    returned, key_sums = attend(received, per_owner)
     arrived = lax.all_to_all(returned, "seq", split_axis=1, concat_axis=1, tiled=True)
     picked = arrived.reshape(heads * CLUSTERS * MOST, 3 * HD)[flat_index].reshape(
         heads, frames, 3 * HD
@@ -107,13 +99,7 @@
     query_grad = join_heads(picked[:, :, :HD])
     key_grad = join_heads(picked[:, :, HD : 2 * HD])
     value_grad = join_heads(picked[:, :, 2 * HD :])
-    member_low = member.astype(jnp.bfloat16)
-    local_sums = jnp.einsum(
-        "htc,htd->chd", member_low, key_heads, preferred_element_type=jnp.float32
-    )
-    centroid_sums = lax.psum_scatter(
-        local_sums.reshape(CLUSTERS, heads * HD), "seq", scatter_dimension=0, tiled=True
-    )
+    centroid_sums = key_sums.transpose(1, 0, 2).reshape(per_owner, heads * HD)
     return (query_grad, key_grad, value_grad, centroid_sums)
 
 

time: 508 us -> 197 us (0.39)
  waiting for transfers between devices: 389 us -> 108 us
  starting transfers between devices: 46.5 us -> 30.9 us
  between operations: 15 us -> 0.93 us
    unnamed x2 -> x0, waiting for transfers between devices: 336 us -> none
    all_to_all x1, waiting for transfers between devices: 0.01 us -> 53.4 us  [shards(): lax.all_to_all(returned, 'seq', split_axis=1, concat_axis=1, tiled=True)]
    all_to_all x1 -> x0, starting transfers between devices: 20.5 us -> none  [shards(): lax.all_to_all(sent_counts, 'seq', split_axis=1, concat_axis=1, tiled=True)]
  transfers between devices with their start and end apart: 4 -> 2, of which waited for: 2 -> 2; matrix products, arithmetic and copies ran while one was open for 3% -> 0% of each run, Pallas kernels for 0% -> 0%
where the time goes in v1:
time: 197 us; the launch traced here: 195 us
  waiting for transfers between devices  108 us (55%)
  starting transfers between devices  30.9 us (16%)
  local copies, waits for them, and re-layouts  30.4 us (15%)
  blocking collectives  11.4 us (6%)
  matrix products  9.63 us (5%)
  other arithmetic  3.71 us (2%)
    all_to_all x1, waiting for transfers between devices, shards(): lax.all_to_all(outgoing, 'seq', split_axis=1, concat_axis=1, tiled=True)  54.3 us
    all_to_all x1, waiting for transfers between devices, shards(): lax.all_to_all(returned, 'seq', split_axis=1, concat_axis=1, tiled=True)  53.4 us
    all_to_all x1, starting transfers between devices, shards(): lax.all_to_all(outgoing, 'seq', split_axis=1, concat_axis=1, tiled=True)  22.5 us
    all_gather x1, blocking collectives, shards(): lax.all_gather(out_grad, 'head', axis=1, tiled=True)  11.4 us
    all_to_all x1, starting transfers between devices, shards(): lax.all_to_all(returned, 'seq', split_axis=1, concat_axis=1, tiled=True)  8.48 us
    unnamed x25, local copies, waits for them, and re-layouts  5.84 us
    scatter x1, local copies, waits for them, and re-layouts, shards(): outgoing = jnp.broadcast_to(empty_row, (heads * CLUSTERS * MOST, 4 * HD))...  5.5 us
    gather x1, local copies, waits for them, and re-layouts, shards(): arrived.reshape(heads * CLUSTERS * MOST, 3 * HD)[flat_index]  3.94 us
  transfers between devices with their start and end apart: 2, of which 2 were waited for; matrix products, arithmetic and copies ran while one was open for 0% of the time, Pallas kernels for 0%

profile of v1, /device:TPU:1, one launch (start us, length us, event | category | flops | bytes accessed | tf_op | source)
XLA Modules:
  0.0 195.2 jit_solution(12251220001705283115)
XLA Ops:
  0.7 0.8 copy.88
  1.6 0.9 fusion.18
  2.5 0.5 add_add_fusion
  3.1 0.4 fusion.19
  3.6 0.4 copy-done.1
  4.0 11.4 %all_gather.3 = bf16[256,1024]{1,0:T(8,128)(2,1)S(1)} all-gather(bf16[256,256]{1,0:T(8,128)(2,1)S(1)} %copy-done.1), channel_id=1, replica_groups=mesh['seq'=128,'head'=4] {'head'}, dimensions={1}, use_global_device_ids=true | all-gather | bytes 655360 | tf_op jit(solution)/shard_map/all_gather | solution.py:59
  15.5 0.8 copy-done.3
  16.4 0.8 copy-done.4
  17.3 0.3 convolution_convert_fusion.1
  18.0 5.5 %scatter_fusion = bf16[2048,256]{1,0:T(8,128)(2,1)S(1)} fusion(bf16[2048,256]{1,0:T(8,128)(2,1)S(1)} %broadcast_in_dim.43, s32[1024]{0:T(1024)S(1)} %bitcast.96, bf16[1024,256]{1,0:T(8,128)(2,1)S(1)} %bitcast.87), kind=kCustom, calls=%fused_computation.1 | custom fusion | bytes 1576960 | tf_op jit(solution)/shard_map/scatter | solution.py:86
  23.5 0.3 reshape.133
  23.8 1.4 copy.64
  25.2 22.5 %all-to-all-start = ((bf16[4,128,4,256]{3,2,0,1:T(4,128)(2,1)}), bf16[4,128,4,256]{3,2,0,1:T(4,128)(2,1)S(1)}, u32[]{:S(2)}, u32[]{:S(2)}) async-start(bf16[4,128,4,256]{3,2,0,1:T(4,128)(2,1)} %copy.64), calls=%async_computation | async-start | bytes 2097152 | tf_op jit(solution)/shard_map/all_to_all | solution.py:89
  47.6 54.3 %all-to-all-done = bf16[4,128,4,256]{3,2,0,1:T(4,128)(2,1)S(1)} async-done(((bf16[4,128,4,256]{3,2,0,1:T(4,128)(2,1)}), bf16[4,128,4,256]{3,2,0,1:T(4,128)(2,1)S(1)}, u32[]{:S(2)}, u32[]{:S(2)}) %all-to-all-start) | async-done | bytes 1048608 | tf_op jit(solution)/shard_map/all_to_all | solution.py:89
  102.0 0.3 copy.65
  102.3 1.1 copy.66
  103.4 0.4 reshape.135
  103.8 0.4 compare_reduce_fusion
  104.2 12.2 %while.10 = (s32[]{:T(128)}, bf16[8,256,192]{1,2,0:T(8,128)(2,1)S(1)}, pred[8,256]{1,0:T(8,128)(4,1)S(1)}, bf16[8,256,256]{2,1,0:T(8,128)(2,1)S(1)}, s32[]{:T(128)}) while((s32[]{:T(128)}, bf16[8,256,192]{1,2,0:T(8,128)(2,1)S(1)}, pred[8,256]{1,0:T(8,128)(4,1)S(1)}, bf16[8,256,256]{2,1,0:T(8,128)(2,1)S(1)}, s32[]{:T(128)}) %tuple.33), condition=%wide.region_8.9_spmd, body=%wide.region_4.8_spmd.sunk | while | flops 51608832 | bytes 2959433 | solution.py:44
  116.4 0.5 copy.68
  117.0 1.4 reshape.136
  118.3 2.5 %copy.69 = bf16[4,128,2,2,192]{1,4,3,2,0:T(8,128)(2,1)S(1)} copy(bf16[4,128,2,2,192]{4,3,1,2,0:T(2,128)(2,1)} %bitcast.83) | data formatting | bytes 1572864 | tf_op jit(solution)/shard_map/transpose | solution.py:45
  120.8 1.7 copy.70
  122.5 8.5 %all-to-all-start.1 = ((bf16[4,128,4,192]{3,2,0,1:T(4,128)(2,1)}), bf16[4,128,4,192]{3,2,0,1:T(4,128)(2,1)S(1)}, u32[]{:S(2)}, u32[]{:S(2)}) async-start(bf16[4,128,4,192]{3,2,0,1:T(4,128)(2,1)} %copy.70), calls=%async_computation.1 | async-start | bytes 2097152 | tf_op jit(solution)/shard_map/all_to_all | solution.py:91
  131.2 0.7 reshape.144
  131.9 53.4 %all-to-all-done.1 = bf16[4,128,4,192]{3,2,0,1:T(4,128)(2,1)S(1)} async-done(((bf16[4,128,4,192]{3,2,0,1:T(4,128)(2,1)}), bf16[4,128,4,192]{3,2,0,1:T(4,128)(2,1)S(1)}, u32[]{:S(2)}, u32[]{:S(2)}) %all-to-all-start.1) | async-done | bytes 786464 | tf_op jit(solution)/shard_map/all_to_all | solution.py:91
  185.3 1.4 copy.71
  186.7 1.7 reshape.138
  188.4 3.9 %gather_fusion = bf16[1024,192]{1,0:T(8,128)(2,1)S(1)} fusion(bf16[2048,192]{1,0:T(8,128)(2,1)S(1)} %reshape.138, s32[1024]{0:T(1024)S(1)} %broadcast_clamp_fusion), kind=kCustom, calls=%fused_computation | custom fusion | bytes 790528 | tf_op jit(solution)/shard_map/gather | solution.py:92
  192.7 0.8 copy.76
  193.6 0.8 copy.77
  194.5 0.8 copy.78
  (131 shorter events, 13.6 us)
Async XLA Ops:
  0.6 16.7 %copy-start = (bf16[256,1024]{1,0:T(8,128)(2,1)S(1)}, bf16[256,1024]{1,0:T(8,128)(2,1)}, u32[]{:S(2)}) copy-start(bf16[256,1024]{1,0:T(8,128)(2,1)} %param.12) | copy-start | bytes 1572868
  0.7 0.8 copy-start.5
  3.1 0.9 copy-start.1
  4.0 11.4 %copy-start.2 = (bf16[256,256]{1,0:T(8,128)(2,1)S(1)}, bf16[256,256]{1,0:T(8,128)(2,1)}, u32[]{:S(2)}) copy-start(bf16[256,256]{1,0:T(8,128)(2,1)} %param.9) | copy-start | bytes 393220
  15.4 0.9 copy-start.3
  16.3 0.9 copy-start.4
  25.2 76.8 %all-to-all-start = ((bf16[4,128,4,256]{3,2,0,1:T(4,128)(2,1)}), bf16[4,128,4,256]{3,2,0,1:T(4,128)(2,1)S(1)}, u32[]{:S(2)}, u32[]{:S(2)}) async-start(bf16[4,128,4,256]{3,2,0,1:T(4,128)(2,1)} %copy.64), calls=%async_computation | async-start | bytes 2097152 | tf_op jit(solution)/shard_map/all_to_all | solution.py:89
  122.5 62.8 %all-to-all-start.1 = ((bf16[4,128,4,192]{3,2,0,1:T(4,128)(2,1)}), bf16[4,128,4,192]{3,2,0,1:T(4,128)(2,1)S(1)}, u32[]{:S(2)}, u32[]{:S(2)}) async-start(bf16[4,128,4,192]{3,2,0,1:T(4,128)(2,1)} %copy.70), calls=%async_computation.1 | async-start | bytes 2097152 | tf_op jit(solution)/shard_map/all_to_all | solution.py:91

commit v2 on v1

v2 whole, which is shorter than its diff:
```python
import functools

import jax
import jax.numpy as jnp
from jax import lax
from jax.experimental import pallas as pl
from jax.experimental.pallas import tpu as pltpu
from jax.sharding import PartitionSpec as P

HD = 64
CLUSTERS = 256
EMPTY = 64.0
MESH = pl.DeviceIdType.MESH
BF = jnp.bfloat16
F32 = jnp.float32
NZ = 16
NXC = 8
NY = 4
CAP = 64
HALF = 32


def iota(shape, dim):
    return lax.broadcasted_iota(jnp.int32, shape, dim)


def onehot(cond):
    return jnp.where(cond, 1.0, 0.0).astype(BF)


def nn(a, b):
    return jnp.dot(a, b, preferred_element_type=F32)


def nt(a, b):
    return lax.dot_general(a, b, (((1,), (1,)), ((), ())), preferred_element_type=F32)


def tn(a, b):
    return lax.dot_general(a, b, (((0,), (0,)), ((), ())), preferred_element_type=F32)


def swap_halves(x):
    return jnp.concatenate([x[:, HD:], x[:, :HD]], axis=1)


def cluster_block(qk, vg):
    low = iota((256, 2 * HD), 1) < HD
    q, k = qk[:, :HD], qk[:, HD:]
    v, g = vg[:, :HD], vg[:, HD:]
    live = qk[:, 0:1].astype(F32) < EMPTY / 2
    scores = jnp.where(live, 0.125 * nt(k, q), jnp.float32(-1e30))
    expo = jnp.exp(scores - jnp.max(scores, axis=0, keepdims=True))
    probs = expo / jnp.sum(expo, axis=0, keepdims=True)
    probs_low = probs.astype(BF)
    dprobs = nt(v, g)
    delta = jnp.sum(probs_low.astype(F32) * dprobs, axis=0, keepdims=True)
    dscores = (probs * (dprobs - delta)).astype(BF)
    dk = 0.125 * nn(dscores, qk)
    dq = 0.125 * tn(dscores, qk)
    dv = nn(probs_low, vg)
    return jnp.where(low, dk, dq).astype(BF), jnp.where(low, swap_halves(dv), dv).astype(BF)


def kernel(
    q_ref, k_ref, v_ref, og_ref, w_ref, ids_ref,
    dq_ref, dk_ref, dv_ref, cs_ref,
    ogr, meta_s, meta_r, zqk_s, zqk_r, zvg_s, zvg_r, xs, xr, yb, zb, xbs, xbr,
    zbqk_s, zbqk_r, zbdv_s, zbdv_r, tcol, tslot,
    sem_s, sem_r, sem_l,
):
    me, hd = lax.axis_index("seq"), lax.axis_index("head")
    x, z, c = me // (2 * NZ), (me // 2) % NZ, me % 2
    xc = x * 2 + c

    def zpeer(i):
        to = (z + i) % NZ
        return to, (x * (2 * NZ) + to * 2 + c, hd)

    def xpeer(i):
        to = (xc + i) % NXC
        return to, ((to // 2) * (2 * NZ) + z * 2 + to % 2, hd)

    def ypeer(i):
        return (me, (hd + i) % NY)

    zorder = [8, 7, 9, 6, 10, 5, 11, 4, 12, 3, 13, 2, 14, 1, 15]
    barrier = pltpu.get_barrier_semaphore()
    peers = [ypeer(i) for i in range(1, NY)]
    peers += [zpeer(i)[1] for i in range(1, NZ)] + [xpeer(i)[1] for i in range(1, NXC)]
    for peer in peers:
        pl.semaphore_signal(barrier, inc=1, device_id=peer, device_id_type=MESH)

    sub, lane = iota((256, 256), 0), iota((256, 256), 1)
    earlier = onehot(sub < lane)
    ones = jnp.ones((256, 256), BF)
    group = sub // 16 == lane // 16
    before = onehot(group & (lane < sub))
    upto_pair = onehot(group & (lane // 2 <= sub // 2))
    before_pair = onehot(group & (lane // 2 < sub // 2))
    member, count, zof = [], [], []
    for h in range(4):
        ids = ids_ref[h : h + 1, :]
        row = ((ids >> 2) & 15) * 16 + (ids >> 6) * 4 + (ids & 3)
        zof.append((row >> 4).astype(F32))
        member.append(onehot(sub == row))
        count.append(nn(member[h], ones).astype(BF))
    targets = []
    meta = jnp.zeros((8, 128), F32)
    mrow = iota((8, 128), 0)
    for h in range(4):
        other = nn(before_pair if h % 2 == 0 else upto_pair, count[h ^ 1])
        place = nn(before, count[h]) + other + nn(member[h], earlier)
        pos = jnp.sum(member[h].astype(F32) * place, axis=0, keepdims=True)
        fits = pos < CAP
        lower = pos < HALF
        targets.append(jnp.where(fits, zof[h] * CAP + pos, -1.0))
        targets.append(jnp.where(lower, zof[h] * HALF + pos, -1.0))
        targets.append(jnp.where(fits & (pos >= HALF), zof[h] * HALF + pos - HALF, -1.0))
        held = nt(jnp.ones((8, 256), BF), member[h])
        meta = jnp.where(mrow == 2 * h, held[:, :128], meta)
        meta = jnp.where(mrow == 2 * h + 1, held[:, 128:], meta)
    meta_s[...] = meta.astype(BF)
    meta_r[pl.ds(z, 1)] = meta.astype(BF)[None]
    tcol[...] = jnp.concatenate(targets + [jnp.zeros((128 - 12, 256), F32)], axis=0).T

    def beside(a_ref, b, p):
        a = a_ref[:, p * 128 : (p + 1) * 128].astype(F32)
        b = b[:, p * 128 : (p + 1) * 128].astype(F32)
        low = iota((256, 128), 1) < HD
        return (
            jnp.where(low, a, swap_halves(b)).astype(BF),
            jnp.where(low, swap_halves(a), b).astype(BF),
        )

    def pack(pair, p, out):
        both = jnp.concatenate(pair, axis=0)
        goal = jnp.concatenate([targets[6 * p], targets[6 * p + 3]], axis=1).astype(jnp.int32)
        step = 4 * CAP
        for part in range(4):
            pick = onehot(iota((step, 512), 0) + part * step == goal)
            rows = nn(pick, both).astype(BF)
            out[p, part * 4 : part * 4 + 4] = rows.reshape(4, CAP, 128)

    pl.semaphore_wait(barrier, NY - 1 + NZ - 1 + NXC - 1)

    def remote(src, dst, sem, peer):
        pltpu.make_async_remote_copy(
            src_ref=src, dst_ref=dst, send_sem=sem_s.at[sem], recv_sem=sem_r.at[sem],
            device_id=peer, device_id_type=MESH,
        ).start()

    def settle(buf, n, sem, which):
        part = buf.at[pl.ds(0, n)]
        pltpu.make_async_copy(part, part, which.at[sem]).wait()

    for i in range(1, NY):
        remote(og_ref, ogr.at[hd], 0, ypeer(i))
    for i in zorder:
        remote(meta_s, meta_r.at[z], 1, zpeer(i)[1])

    def send_z(src, dst, p, sem):
        for i in zorder:
            to, peer = zpeer(i)
            remote(src.at[p, to], dst.at[p, z], sem, peer)
        own = pltpu.make_async_copy(src.at[p, z], dst.at[p, z], sem_l.at[sem])
        own.start()

    def wait_z(src, dst, p, sem):
        settle(dst.at[p], NZ - 1, sem, sem_r)
        pltpu.make_async_copy(src.at[p, z], dst.at[p, z], sem_l.at[sem]).wait()

    def send_x(src, dst, p, sem):
        for i in range(1, NXC):
            to, peer = xpeer(i)
            remote(src.at[p, to], dst.at[p, xc], sem, peer)
        pltpu.make_async_copy(src.at[p, xc], dst.at[p, xc], sem_l.at[sem]).start()

    def wait_x(src, dst, p, sem):
        settle(dst.at[p], NXC - 1, sem, sem_r)
        pltpu.make_async_copy(src.at[p, xc], dst.at[p, xc], sem_l.at[sem]).wait()

    pack(beside(q_ref, k_ref, 0), 0, zqk_s)
    send_z(zqk_s, zqk_r, 0, 2)
    qk_b = beside(q_ref, k_ref, 1)
    settle(ogr, NY - 1, 0, sem_r)
    grad = jnp.zeros((256, 256), F32)
    for i in range(NY):
        y = (hd + i) % NY
        piece = og_ref[...] if i == 0 else ogr[pl.ds(y, 1)][0]
        grad += nt(piece, w_ref[pl.ds(y, 1)][0])
    d_out = grad.astype(BF)
    pack(beside(v_ref, d_out, 0), 0, zvg_s)
    send_z(zvg_s, zvg_r, 0, 4)
    pack(qk_b, 1, zqk_s)
    send_z(zqk_s, zqk_r, 1, 3)
    pack(beside(v_ref, d_out, 1), 1, zvg_s)
    send_z(zvg_s, zvg_r, 1, 5)

    settle(meta_r, NZ - 1, 1, sem_r)
    r_i, l_i = iota((128, 128), 0), iota((128, 128), 1)
    slot_row = (l_i // 8) * 2 + (l_i // 2) % 2
    select = onehot((r_i % 16 == slot_row) & (r_i // 16 == z % 8) & (l_i < 64))
    found = nn(meta_r[...].reshape(128, 128), select)
    half = r_i % 2 == z // 8
    smaller = onehot(r_i < l_i)
    l16 = iota((16, 128), 1)
    for p in range(2):
        mine = jnp.where(half & ((r_i // 2) % 4 == 2 * p + (l_i // 4) % 2), found, 0.0)
        held = jnp.sum(mine.reshape(16, 8, 128), axis=1)
        taken = held > (l16 % 2).astype(F32)
        ahead = nn(onehot(taken), smaller)
        tslot[p] = jnp.where(taken, ahead, float(CAP))

    s_i, o_i = iota((256, 256), 0), iota((256, 256), 1)

    def source(o):
        return ((o // 2) % 16) * 16 + (o // 128) * 8 + ((o // 32) % 4) * 2 + o % 2

    perm = onehot(o_i == source(s_i))
    perm_back = onehot(s_i == source(o_i))
    mark = jnp.where((iota((16, 256), 0) == 0) & (iota((16, 256), 1) == 0), EMPTY, 0.0)
    mark = mark.astype(BF)

    def expand(p):
        for s in range(NZ):
            slot = tslot[p, s : s + 1, 0:64].astype(jnp.int32)
            pick = onehot(iota((CAP + 16, 64), 0) == slot)
            rows = jnp.concatenate([zqk_r[p, s], zvg_r[p, s]], axis=1)
            rows = tn(pick, jnp.concatenate([rows, mark], axis=0))
            rows = [rows[:, :128].reshape(8, 8, 128), rows[:, 128:].reshape(8, 8, 128)]
            xs[p, :, s] = jnp.concatenate(rows, axis=1).astype(BF)

    def work(p):
        for i in range(NXC):
            rows = nn(perm, xr[p, i].reshape(256, 128)).astype(BF)
            for b in range(8):
                yb[b, i * 32 : (i + 1) * 32, :] = rows[b * 32 : (b + 1) * 32]
        sums = []
        for b in range(4):
            zb[b], zb[4 + b] = cluster_block(yb[b], yb[4 + b])
            sums.append(jnp.sum(yb[b].astype(F32), axis=0, keepdims=True))
        for j in range(2):
            cs_ref[j : j + 1, p * 128 : (p + 1) * 128] = jnp.concatenate(
                [sums[j][:, HD:], sums[2 + j][:, HD:]], axis=1
            )
        for i in range(NXC):
            rows = [zb[b, i * 32 : (i + 1) * 32, :] for b in range(8)]
            rows = nn(perm_back, jnp.concatenate(rows, axis=0)).astype(BF)
            xbs[p, i] = rows.reshape(16, 16, 128)

    def compact(p):
        low = iota((HALF, 128), 1) < HD
        for s in range(NZ):
            slot = tslot[p, s : s + 1, 0:64].astype(jnp.int32)
            back = xbr[p, :, s].astype(F32)
            bqk = back[:, :8].reshape(64, 128).astype(BF)
            bdv = back[:, 8:].reshape(64, 128).astype(BF)
            zbqk_s[p, s] = nn(onehot(iota((CAP, 64), 0) == slot), bqk).astype(BF)
            at = iota((HALF, 64), 0)
            first = nn(onehot(at == slot), bdv)
            second = nn(onehot((at + HALF == slot) & (slot < CAP)), bdv)
            zbdv_s[p, s] = jnp.where(low, first, second).astype(BF)

    def unpack(p):
        keys, values, queries = [], [], []
        for h in (2 * p, 2 * p + 1):
            def pick(k, n):
                col = tcol[:, 3 * h + k : 3 * h + k + 1].astype(jnp.int32)
                return onehot(iota((256, NZ * n), 1) == col)

            got = nn(pick(0, CAP), zbqk_r[p].reshape(NZ * CAP, 128))
            dv_rows = zbdv_r[p].reshape(NZ * HALF, 128)
            first, second = nn(pick(1, HALF), dv_rows), nn(pick(2, HALF), dv_rows)
            keys.append(got[:, :HD])
            queries.append(got[:, HD:])
            values.append(first[:, :HD] + second[:, HD:])
        for ref, parts in ((dq_ref, queries), (dk_ref, keys), (dv_ref, values)):
            ref[:, p * 128 : (p + 1) * 128] = jnp.concatenate(parts, axis=1).astype(BF)

    def wait_rows(p):
        wait_z(zqk_s, zqk_r, p, 2 + p)
        wait_z(zvg_s, zvg_r, p, 4 + p)

    def send_back(p):
        wait_x(xbs, xbr, p, 8 + p)
        compact(p)
        send_z(zbqk_s, zbqk_r, p, 10 + p)
        send_z(zbdv_s, zbdv_r, p, 12 + p)

    wait_rows(0)
    expand(0)
    send_x(xs, xr, 0, 6)
    wait_x(xs, xr, 0, 6)
    work(0)
    send_x(xbs, xbr, 0, 8)
    wait_rows(1)
    expand(1)
    send_x(xs, xr, 1, 7)
    send_back(0)
    wait_x(xs, xr, 1, 7)
    work(1)
    send_x(xbs, xbr, 1, 9)
    send_back(1)
    for p in range(2):
        wait_z(zbqk_s, zbqk_r, p, 10 + p)
        wait_z(zbdv_s, zbdv_r, p, 12 + p)
        unpack(p)

    for i in range(1, NY):
        pltpu.make_async_copy(og_ref, og_ref, sem_s.at[0]).wait()
    for i in range(1, NZ):
        pltpu.make_async_copy(meta_s, meta_s, sem_s.at[1]).wait()
    for p in range(2):
        settle(zqk_s.at[p], NZ - 1, 2 + p, sem_s)
        settle(zvg_s.at[p], NZ - 1, 4 + p, sem_s)
        settle(xs.at[p], NXC - 1, 6 + p, sem_s)
        settle(xbs.at[p], NXC - 1, 8 + p, sem_s)
        settle(zbqk_s.at[p], NZ - 1, 10 + p, sem_s)
        settle(zbdv_s.at[p], NZ - 1, 12 + p, sem_s)


def shards(queries, keys, values, out_grad, w_out, cluster_ids):
    frames, width = queries.shape
    heads = cluster_ids.shape[0]
    vmem = pl.BlockSpec(memory_space=pltpu.VMEM)
    grad = jax.ShapeDtypeStruct((frames, width), BF)

    def buf(*shape):
        return pltpu.VMEM(shape, BF)

    w_parts = w_out.reshape(width, NY, width).transpose(1, 0, 2)
    return pl.pallas_call(
        kernel,
        name="routed_attention",
        out_shape=(grad, grad, grad, jax.ShapeDtypeStruct((2, width), F32)),
        in_specs=[vmem] * 6,
        out_specs=(vmem,) * 4,
        scratch_shapes=[
            buf(NY, frames, width),
            buf(8, 128),
            buf(NZ, 8, 128),
            buf(2, NZ, CAP, 128),
            buf(2, NZ, CAP, 128),
            buf(2, NZ, CAP, 128),
            buf(2, NZ, CAP, 128),
            buf(2, NXC, NZ, 16, 128),
            buf(2, NXC, NZ, 16, 128),
            buf(8, 256, 128),
            buf(8, 256, 128),
            buf(2, NXC, NZ, 16, 128),
            buf(2, NXC, NZ, 16, 128),
            buf(2, NZ, CAP, 128),
            buf(2, NZ, CAP, 128),
            buf(2, NZ, HALF, 128),
            buf(2, NZ, HALF, 128),
            pltpu.VMEM((256, 128), F32),
            pltpu.VMEM((2, NZ, 128), F32),
            pltpu.SemaphoreType.DMA((14,)),
            pltpu.SemaphoreType.DMA((14,)),
            pltpu.SemaphoreType.DMA((14,)),
        ],
        compiler_params=pltpu.CompilerParams(
            collective_id=0, has_side_effects=True, vmem_limit_bytes=48 << 20
        ),
    )(queries, keys, values, out_grad, w_parts, cluster_ids.reshape(heads, frames))


def solution(mesh):
    placed = (
        P("seq", "head"),
        P("seq", "head"),
        P("seq", "head"),
        P("seq", "head"),
        P("head", None),
        P("head", "seq", None),
    )
    return jax.shard_map(
        shards,
        mesh=mesh,
        in_specs=placed,
        out_specs=(P("seq", "head"), P("seq", "head"), P("seq", "head"), P("seq", "head")),
        check_vma=False,
    )
```

time: 197 us -> 110 us (0.56)
  waiting for transfers between devices: 108 us -> 0 us
  Pallas kernels: 0 us -> 104 us
  starting transfers between devices: 30.9 us -> 0 us
  local copies, waits for them, and re-layouts: 30.4 us -> 4.86 us
  blocking collectives: 11.4 us -> 0 us
  matrix products: 9.63 us -> 0 us
  other arithmetic: 3.71 us -> 0 us
    all_to_all x2 -> x0, waiting for transfers between devices: 108 us -> none  [the longest x1 54.3 us: shards(): lax.all_to_all(outgoing, 'seq', split_axis=1, concat_axis=1, tiled=True)]
    pallas_call x0 -> x1, Pallas kernels: none -> 104 us  [shards(): pl.pallas_call(kernel, name='routed_attention', out_shape=(grad, grad, gr...]
    all_to_all x2 -> x0, starting transfers between devices: 30.9 us -> none  [the longest x1 22.5 us: shards(): lax.all_to_all(outgoing, 'seq', split_axis=1, concat_axis=1, tiled=True)]
    all_gather x1 -> x0, blocking collectives: 11.4 us -> none  [shards(): lax.all_gather(out_grad, 'head', axis=1, tiled=True)]
    dot_general x49 -> x0, matrix products: 9.63 us -> none  [the longest x8 2.05 us: cluster_block(): jnp.dot(q_rows, k_rows.T, preferred_element_type=jnp.float32)]
    reshape x7 -> x1, local copies, waits for them, and re-layouts: 7.52 us -> 0.2 us  [shards(): w_parts = w_out.reshape(width, NY, width).transpose(1, 0, 2)]
    scatter x1 -> x0, local copies, waits for them, and re-layouts: 5.5 us -> none  [shards(): outgoing = jnp.broadcast_to(empty_row, (heads * CLUSTERS * MOST, 4 * HD))...]
    gather x1 -> x0, local copies, waits for them, and re-layouts: 3.94 us -> none  [shards(): arrived.reshape(heads * CLUSTERS * MOST, 3 * HD)[flat_index]]
  transfers between devices with their start and end apart: 2 -> 0, of which waited for: 2 -> 0; matrix products, arithmetic and copies ran while one was open for 0% -> 0% of each run, Pallas kernels for 0% -> 0%
where the time goes in v2:
time: 110 us
  Pallas kernels  104 us (95%)
  local copies, waits for them, and re-layouts  4.86 us (4%)
    pallas_call x1, Pallas kernels, shards(): pl.pallas_call(kernel, name='routed_attention', out_shape=(grad, grad, gr...  104 us
    unnamed x16, local copies, waits for them, and re-layouts  4.66 us

profile of v2, /device:TPU:1, one launch (start us, length us, event | category | flops | bytes accessed | tf_op | source)
XLA Modules:
  0.0 109.9 jit_solution(4145100102436666491)
XLA Ops:
  0.6 1.2 %copy.10 = bf16[256,1024]{0,1:T(8,128)(2,1)S(1)} copy(bf16[256,1024]{1,0:T(8,128)(2,1)} %param.10) | data formatting | bytes 1048576 | tf_op args[4]
  1.9 0.0 copy-start.4
  1.9 0.0 copy-start
  1.9 0.0 copy-start.1
  1.9 0.0 copy-start.2
  1.9 0.0 copy-start.3
  1.9 0.2 copy.11
  2.1 0.4 copy-done.4
  2.6 0.2 copy-done
  2.8 0.1 copy-done.1
  2.9 0.1 copy-done.2
  2.9 0.1 copy-done.3
  3.0 104.3 %routed_attention.1 = (bf16[256,256]{1,0:T(8,128)(2,1)S(1)}, bf16[256,256]{1,0:T(8,128)(2,1)S(1)}, bf16[256,256]{1,0:T(8,128)(2,1)S(1)}, f32[2,256]{1,0:T(2,128)S(1)}) custom-call(bf16[256,256]{1,0:T(8,128)(2,1)S(1)} %copy-done, bf16[256,256]{1,0:T(8,128)(2,1)S(1)} %copy-done.1, bf16[256,256]{1,0:T(8,128)(2,1)S(1)} %copy-done.2, ...), custom_call_target="tpu_custom_call" | custom-call | tf_op jit(solution)/shard_map/routed_attention/pallas_call | solution.py:333
  107.3 0.7 copy.19
  108.0 0.7 copy.20
  108.6 0.7 copy.21
  109.3 0.6 copy.22
  (1 shorter events, 0.0 us)
Async XLA Ops:
  1.9 0.7 copy-start.4
  1.9 0.9 copy-start
  1.9 1.0 copy-start.1
  1.9 1.0 copy-start.2
  1.9 1.1 copy-start.3

commit v3 on v2

v3 whole, which is shorter than its diff:
```python
import functools

import jax
import jax.numpy as jnp
from jax import lax
from jax.experimental import pallas as pl
from jax.experimental.pallas import tpu as pltpu
from jax.sharding import PartitionSpec as P

HD = 64
CLUSTERS = 256
MOST = 2
EMPTY = 64.0
MESH = pl.DeviceIdType.MESH
BF = jnp.bfloat16
F32 = jnp.float32
NZ = 16
NXC = 8
NY = 4
CAP = 40
HALF = 24
ROWS = 2 * CAP
BACK = CAP + HALF
NONE = float(ROWS)


def iota(shape, dim):
    return lax.broadcasted_iota(jnp.int32, shape, dim)


def onehot(cond):
    return jnp.where(cond, 1.0, 0.0).astype(BF)


def nn(a, b):
    return jnp.dot(a, b, preferred_element_type=F32)


def nt(a, b):
    return lax.dot_general(a, b, (((1,), (1,)), ((), ())), preferred_element_type=F32)


def tn(a, b):
    return lax.dot_general(a, b, (((0,), (0,)), ((), ())), preferred_element_type=F32)


def swap_halves(x):
    return jnp.concatenate([x[:, HD:], x[:, :HD]], axis=1)


def cluster_block(qk, vg):
    low = iota((256, 2 * HD), 1) < HD
    q, k = qk[:, :HD], qk[:, HD:]
    v, g = vg[:, :HD], vg[:, HD:]
    live = qk[:, 0:1].astype(F32) < EMPTY / 2
    scores = jnp.where(live, 0.125 * nt(k, q), jnp.float32(-1e30))
    expo = jnp.exp(scores - jnp.max(scores, axis=0, keepdims=True))
    probs = expo / jnp.sum(expo, axis=0, keepdims=True)
    probs_low = probs.astype(BF)
    dprobs = nt(v, g)
    delta = jnp.sum(probs_low.astype(F32) * dprobs, axis=0, keepdims=True)
    dscores = (probs * (dprobs - delta)).astype(BF)
    dk = 0.125 * nn(dscores, qk)
    dq = 0.125 * tn(dscores, qk)
    dv = nn(probs_low, vg)
    return jnp.where(low, dk, dq).astype(BF), jnp.where(low, swap_halves(dv), dv).astype(BF)


def kernel(
    q_ref, k_ref, v_ref, og_ref, w_ref, ids_ref,
    dq_ref, dk_ref, dv_ref, cs_ref, full_ref,
    ogr, meta_s, meta_r, zs, zr, xs, xr, yb, zb, xbs, xbr, zbs, zbr, tcol, tslot,
    sum_own, sum_s, sum_r, full_xs, full_xr, full_ys, full_yr,
    sem_s, sem_r, sem_l,
):
    me, hd = lax.axis_index("seq"), lax.axis_index("head")
    x, z, c = me // (2 * NZ), (me // 2) % NZ, me % 2
    xc = x * 2 + c

    def zpeer(i):
        to = (z + i) % NZ
        return to, (x * (2 * NZ) + to * 2 + c, hd)

    def xpeer(i):
        to = (xc + i) % NXC
        return to, ((to // 2) * (2 * NZ) + z * 2 + to % 2, hd)

    def ypeer(i):
        return (me, (hd + i) % NY)

    zorder = [8, 7, 9, 6, 10, 5, 11, 4, 12, 3, 13, 2, 14, 1, 15]
    barrier = pltpu.get_barrier_semaphore()
    peers = [ypeer(i) for i in range(1, NY)]
    peers += [zpeer(i)[1] for i in range(1, NZ)] + [xpeer(i)[1] for i in range(1, NXC)]
    for peer in peers:
        pl.semaphore_signal(barrier, inc=1, device_id=peer, device_id_type=MESH)

    sub, lane = iota((256, 256), 0), iota((256, 256), 1)
    earlier = onehot(sub < lane)
    ones = jnp.ones((256, 256), BF)
    group = sub // 16 == lane // 16
    before = onehot(group & (lane < sub))
    across = sub // 16 == (lane // 16 + NZ // 2) % NZ
    upto_pair = onehot(across & ((lane % 16) // 2 <= (sub % 16) // 2))
    before_pair = onehot(across & ((lane % 16) // 2 < (sub % 16) // 2))
    member, count, zof = [], [], []
    for h in range(4):
        ids = ids_ref[h : h + 1, :]
        row = ((ids >> 2) & 15) * 16 + (ids >> 6) * 4 + (ids & 3)
        zof.append((((row >> 4) + (h % 2) * (NZ // 2)) & (NZ - 1)).astype(F32))
        member.append(onehot(sub == row))
        count.append(nn(member[h], ones).astype(BF))
    targets = []
    meta = jnp.zeros((8, 128), F32)
    mrow = iota((8, 128), 0)
    for h in range(4):
        other = nn(before_pair if h % 2 == 0 else upto_pair, count[h ^ 1])
        place = nn(before, count[h]) + other + nn(member[h], earlier)
        pos = jnp.sum(member[h].astype(F32) * place, axis=0, keepdims=True)
        fits = pos < CAP
        lower = pos < HALF
        targets.append(jnp.where(fits, zof[h] * CAP + pos, -1.0))
        back = zof[h] * BACK + pos
        targets.append(jnp.where(fits, back, -1.0))
        targets.append(jnp.where(lower, back + CAP, -1.0))
        targets.append(jnp.where(fits & (pos >= HALF), back + CAP - HALF, -1.0))
        held = nt(jnp.ones((8, 256), BF), member[h])
        meta = jnp.where(mrow == 2 * h, held[:, :128], meta)
        meta = jnp.where(mrow == 2 * h + 1, held[:, 128:], meta)
    meta_s[...] = meta.astype(BF)
    meta_r[pl.ds(z, 1)] = meta.astype(BF)[None]
    tcol[...] = jnp.concatenate(targets + [jnp.zeros((128 - 16, 256), F32)], axis=0).T

    def beside(a_ref, b, p):
        a = a_ref[:, p * 128 : (p + 1) * 128].astype(F32)
        b = b[:, p * 128 : (p + 1) * 128].astype(F32)
        low = iota((256, 128), 1) < HD
        return (
            jnp.where(low, a, swap_halves(b)).astype(BF),
            jnp.where(low, swap_halves(a), b).astype(BF),
        )

    def pack(pair, p, at):
        both = jnp.concatenate(pair, axis=0)
        goal = jnp.concatenate([targets[8 * p], targets[8 * p + 4]], axis=1).astype(jnp.int32)
        step = 4 * CAP
        for part in range(4):
            pick = onehot(iota((step, 512), 0) + part * step == goal)
            rows = nn(pick, both).reshape(4, CAP, 128).astype(BF)
            zs[p, part * 4 : part * 4 + 4, at : at + CAP, :] = rows

    pl.semaphore_wait(barrier, NY - 1 + NZ - 1 + NXC - 1)

    def remote(src, dst, sem, peer):
        pltpu.make_async_remote_copy(
            src_ref=src, dst_ref=dst, send_sem=sem_s.at[sem], recv_sem=sem_r.at[sem],
            device_id=peer, device_id_type=MESH,
        ).start()

    def settle(buf, n, sem, which):
        part = buf.at[pl.ds(0, n)]
        pltpu.make_async_copy(part, part, which.at[sem]).wait()

    for i in range(1, NY):
        remote(og_ref, ogr.at[hd], 0, ypeer(i))
    for i in zorder:
        remote(meta_s, meta_r.at[z], 1, zpeer(i)[1])

    def send_z(src, dst, p, sem):
        for i in zorder:
            to, peer = zpeer(i)
            remote(src.at[p, to], dst.at[p, z], sem, peer)
        own = pltpu.make_async_copy(src.at[p, z], dst.at[p, z], sem_l.at[sem])
        own.start()

    def wait_z(src, dst, p, sem):
        settle(dst.at[p], NZ - 1, sem, sem_r)
        pltpu.make_async_copy(src.at[p, z], dst.at[p, z], sem_l.at[sem]).wait()

    def send_x(src, dst, p, sem):
        for i in range(1, NXC):
            to, peer = xpeer(i)
            remote(src.at[p, to], dst.at[p, xc], sem, peer)
        pltpu.make_async_copy(src.at[p, xc], dst.at[p, xc], sem_l.at[sem]).start()

    def wait_x(src, dst, p, sem):
        settle(dst.at[p], NXC - 1, sem, sem_r)
        pltpu.make_async_copy(src.at[p, xc], dst.at[p, xc], sem_l.at[sem]).wait()

    for p in range(2):
        pack(beside(q_ref, k_ref, p), p, 0)
    settle(ogr, NY - 1, 0, sem_r)
    grad = jnp.zeros((256, 256), F32)
    for i in range(NY):
        y = (hd + i) % NY
        piece = og_ref[...] if i == 0 else ogr[pl.ds(y, 1)][0]
        grad += nt(piece, w_ref[:, pl.ds(pl.multiple_of(y * 256, 256), 256)])
    d_out = grad.astype(BF)
    for p in range(2):
        pack(beside(v_ref, d_out, p), p, CAP)
        send_z(zs, zr, p, 2 + p)

    settle(meta_r, NZ - 1, 1, sem_r)
    r_i, l_i = iota((128, 128), 0), iota((128, 128), 1)
    slot_row = (l_i // 8) * 2 + (l_i // 2) % 2
    select = onehot((r_i % 16 == slot_row) & (r_i // 16 == z % 8) & (l_i < 64))
    meta_all = meta_r[...].reshape(128, 128)
    found = nn(meta_all, select)
    half = r_i % 2 == (z // 8 + (l_i // 4) % 2) % 2
    smaller = onehot(r_i < l_i)
    l16 = iota((16, 128), 1)
    for p in range(2):
        mine = jnp.where(half & ((r_i // 2) % 4 == 2 * p + (l_i // 4) % 2), found, 0.0)
        held = jnp.sum(mine.reshape(16, 8, 128), axis=1)
        taken = held > (l16 % 2).astype(F32)
        ahead = nn(onehot(taken), smaller)
        tslot[p] = jnp.where(taken, ahead, NONE)
    pair = (l_i // 8 == r_i // 8) & ((l_i % 8) // 4 == (r_i % 8) // 2)
    pair = pair & ((l_i % 2 + (l_i // 2) % 2) % 2 == r_i % 2)
    places = nn(onehot(pair), meta_all).astype(BF)
    places = nn(places, onehot(r_i // 16 == l_i))
    most = jnp.max(jnp.max(places, axis=0, keepdims=True), axis=1, keepdims=True)
    full = jnp.broadcast_to(jnp.where(most > CAP, 1.0, 0.0), (8, 128))
    full_xs[...] = full
    full_xr[pl.ds(xc, 1)] = full[None]
    for i in range(1, NXC):
        remote(full_xs, full_xr.at[xc], 10, xpeer(i)[1])

    s_i, o_i = iota((256, 256), 0), iota((256, 256), 1)

    def source(o):
        return ((o // 2) % 16) * 16 + (o // 128) * 8 + ((o // 32) % 4) * 2 + o % 2

    perm = onehot(o_i == source(s_i))
    perm_back = onehot(s_i == source(o_i))
    mark = jnp.where((iota((16, 128), 0) == 0) & (iota((16, 128), 1) == 0), EMPTY, 0.0)
    mark = mark.astype(BF)

    def expand(p):
        at = iota((ROWS + 16, 64), 0)
        for s in range(NZ):
            slot = tslot[p, s : s + 1, 0:64].astype(jnp.int32)
            rows = jnp.concatenate([zr[p, s], mark], axis=0)
            qk = tn(onehot(at == slot), rows).reshape(8, 8, 128)
            vg = tn(onehot(at == slot + CAP), rows).reshape(8, 8, 128)
            xs[p, :, s] = jnp.concatenate([qk, vg], axis=1).astype(BF)

    def work(p):
        for i in range(NXC):
            rows = nn(perm, xr[p, i].reshape(256, 128)).astype(BF)
            for b in range(8):
                yb[b, i * 32 : (i + 1) * 32, :] = rows[b * 32 : (b + 1) * 32]
        sums = []
        for b in range(4):
            zb[b], zb[4 + b] = cluster_block(yb[b], yb[4 + b])
            sums.append(jnp.sum(yb[b].astype(F32), axis=0, keepdims=True))
        for j in range(2):
            sum_own[j : j + 1, p * HD : (p + 1) * HD] = sums[j][:, HD:]
            sum_s[j : j + 1, p * HD : (p + 1) * HD] = sums[2 + j][:, HD:]
        for i in range(NXC):
            rows = [zb[b, i * 32 : (i + 1) * 32, :] for b in range(8)]
            rows = nn(perm_back, jnp.concatenate(rows, axis=0)).astype(BF)
            xbs[p, i] = rows.reshape(16, 16, 128)

    def compact(p):
        low = iota((BACK, 128), 1) < HD
        at = iota((BACK, 64), 0)
        for s in range(NZ):
            slot = tslot[p, s : s + 1, 0:64].astype(jnp.int32)
            back = xbr[p, :, s].astype(F32)
            back = [back[:, :8].reshape(64, 128), back[:, 8:].reshape(64, 128)]
            back = jnp.concatenate(back, axis=0).astype(BF)
            qk = at == slot
            lower = (at == slot + CAP) & (slot < HALF)
            upper = (at + HALF == slot + CAP) & (slot >= HALF) & (slot < CAP)
            first = nn(jnp.concatenate([onehot(qk), onehot(lower)], axis=1), back)
            second = nn(jnp.concatenate([onehot(qk), onehot(upper)], axis=1), back)
            zbs[p, s] = jnp.where(low, first, second).astype(BF)

    def unpack(p):
        keys, values, queries = [], [], []
        rows = zbr[p].reshape(NZ * BACK, 128)
        at = iota((256, NZ * BACK), 1)
        for h in (2 * p, 2 * p + 1):
            cols = tcol[:, 4 * h : 4 * h + 4].astype(jnp.int32)
            got = nn(onehot(at == cols[:, 1:2]), rows)
            first = nn(onehot(at == cols[:, 2:3]), rows)
            second = nn(onehot(at == cols[:, 3:4]), rows)
            keys.append(got[:, :HD])
            queries.append(got[:, HD:])
            values.append(first[:, :HD] + second[:, HD:])
        for ref, parts in ((dq_ref, queries), (dk_ref, keys), (dv_ref, values)):
            ref[:, p * 128 : (p + 1) * 128] = jnp.concatenate(parts, axis=1).astype(BF)

    def send_back(p):
        wait_x(xbs, xbr, p, 6 + p)
        compact(p)
        send_z(zbs, zbr, p, 8 + p)

    wait_z(zs, zr, 0, 2)
    expand(0)
    send_x(xs, xr, 0, 4)
    settle(full_xr, NXC - 1, 10, sem_r)
    full = jnp.max(full_xr[...], axis=0)
    full_ys[...] = full
    for i in range(1, NY):
        remote(full_ys, full_yr.at[hd], 11, ypeer(i))
    wait_x(xs, xr, 0, 4)
    work(0)
    send_x(xbs, xbr, 0, 6)
    wait_z(zs, zr, 1, 3)
    expand(1)
    send_x(xs, xr, 1, 5)
    send_back(0)
    wait_x(xs, xr, 1, 5)
    work(1)
    send_x(xbs, xbr, 1, 7)
    remote(sum_s, sum_r, 12, zpeer(NZ // 2)[1])
    send_back(1)
    pltpu.make_async_copy(sum_r, sum_r, sem_r.at[12]).wait()
    for p in range(2):
        cols = slice(p * HD, (p + 1) * HD)
        cs_ref[:, p * 128 : (p + 1) * 128] = jnp.concatenate(
            [sum_own[0:2, cols], sum_r[0:2, cols]], axis=1
        )
    settle(full_yr, NY - 1, 11, sem_r)
    for i in range(1, NY):
        full = jnp.maximum(full, full_yr[pl.ds((hd + i) % NY, 1)][0])
    full_ref[...] = full
    for p in range(2):
        wait_z(zbs, zbr, p, 8 + p)
        unpack(p)

    for i in range(1, NY):
        pltpu.make_async_copy(og_ref, og_ref, sem_s.at[0]).wait()
        pltpu.make_async_copy(full_ys, full_ys, sem_s.at[11]).wait()
    for i in range(1, NZ):
        pltpu.make_async_copy(meta_s, meta_s, sem_s.at[1]).wait()
    for i in range(1, NXC):
        pltpu.make_async_copy(full_xs, full_xs, sem_s.at[10]).wait()
    pltpu.make_async_copy(sum_s, sum_s, sem_s.at[12]).wait()
    for p in range(2):
        settle(zs.at[p], NZ - 1, 2 + p, sem_s)
        settle(xs.at[p], NXC - 1, 4 + p, sem_s)
        settle(xbs.at[p], NXC - 1, 6 + p, sem_s)
        settle(zbs.at[p], NZ - 1, 8 + p, sem_s)


def two_hop(queries, keys, values, out_grad, w_out, cluster_ids):
    frames, width = queries.shape
    heads = cluster_ids.shape[0]
    vmem = pl.BlockSpec(memory_space=pltpu.VMEM)
    grad = jax.ShapeDtypeStruct((frames, width), BF)

    def buf(*shape, dtype=BF):
        return pltpu.VMEM(shape, dtype)

    return pl.pallas_call(
        kernel,
        name="two_hop",
        out_shape=(
            grad, grad, grad,
            jax.ShapeDtypeStruct((2, width), F32), jax.ShapeDtypeStruct((8, 128), F32),
        ),
        in_specs=[vmem] * 6,
        out_specs=(vmem,) * 5,
        scratch_shapes=[
            buf(NY, frames, width),
            buf(8, 128),
            buf(NZ, 8, 128),
            buf(2, NZ, ROWS, 128),
            buf(2, NZ, ROWS, 128),
            buf(2, NXC, NZ, 16, 128),
            buf(2, NXC, NZ, 16, 128),
            buf(8, 256, 128),
            buf(8, 256, 128),
            buf(2, NXC, NZ, 16, 128),
            buf(2, NXC, NZ, 16, 128),
            buf(2, NZ, BACK, 128),
            buf(2, NZ, BACK, 128),
            buf(256, 128, dtype=F32),
            buf(2, NZ, 128, dtype=F32),
            buf(8, 128, dtype=F32),
            buf(8, 128, dtype=F32),
            buf(8, 128, dtype=F32),
            buf(8, 128, dtype=F32),
            buf(NXC, 8, 128, dtype=F32),
            buf(8, 128, dtype=F32),
            buf(NY, 8, 128, dtype=F32),
            pltpu.SemaphoreType.DMA((13,)),
            pltpu.SemaphoreType.DMA((13,)),
            pltpu.SemaphoreType.DMA((13,)),
        ],
        compiler_params=pltpu.CompilerParams(
            collective_id=0, has_side_effects=True, vmem_limit_bytes=48 << 20
        ),
    )(queries, keys, values, out_grad, w_out, cluster_ids.reshape(heads, frames))


def padded_block(block, live):
    q_rows = block[:, :HD]
    k_rows = block[:, HD : 2 * HD]
    v_rows = block[:, 2 * HD : 3 * HD]
    g_rows = block[:, 3 * HD :]
    scores = 0.125 * jnp.dot(q_rows, k_rows.T, preferred_element_type=jnp.float32)
    scores = jnp.where(live[None, :], scores, jnp.float32(-1e30))
    top = jnp.max(scores, axis=1, keepdims=True)
    expo = jnp.exp(scores - top)
    probs = expo / jnp.sum(expo, axis=1, keepdims=True)
    probs_low = probs.astype(jnp.bfloat16)
    attended = jnp.dot(probs_low, v_rows, preferred_element_type=jnp.float32)
    delta = jnp.sum(g_rows.astype(jnp.float32) * attended, axis=1, keepdims=True)
    dprobs = jnp.dot(g_rows, v_rows.T, preferred_element_type=jnp.float32)
    dscores = (probs * (dprobs - delta)).astype(jnp.bfloat16)
    dq_rows = (0.125 * jnp.dot(dscores, k_rows, preferred_element_type=jnp.float32)).astype(
        jnp.bfloat16
    )
    dk_rows = (0.125 * jnp.dot(dscores.T, q_rows, preferred_element_type=jnp.float32)).astype(
        jnp.bfloat16
    )
    dv_rows = jnp.dot(probs_low.T, g_rows, preferred_element_type=jnp.float32).astype(jnp.bfloat16)
    return jnp.concatenate([dq_rows, dk_rows, dv_rows], axis=1)


def padded_attend(received, per_owner):
    count_items = received.shape[0]
    owners = received.shape[1]
    capacity = owners * MOST
    blocks = received.reshape(count_items, owners, per_owner, MOST, 4 * HD)
    blocks = blocks.transpose(0, 2, 1, 3, 4).reshape(count_items * per_owner, capacity, 4 * HD)
    live = blocks[:, :, 0] < EMPTY / 2
    grads = lax.map(lambda pair: padded_block(pair[0], pair[1]), (blocks, live))
    grads = grads.reshape(count_items, per_owner, owners, MOST, 3 * HD).transpose(0, 2, 1, 3, 4)
    returned = grads.reshape(count_items, owners, per_owner * MOST, 3 * HD)
    key_sums = jnp.sum(blocks[:, :, HD : 2 * HD].astype(jnp.float32), axis=1).reshape(
        count_items, per_owner, HD
    )
    return (returned, key_sums)


def padded(queries, keys, values, out_grad, w_out, cluster_ids):
    frames = queries.shape[0]
    heads = cluster_ids.shape[0]
    owners = lax.axis_size("seq")
    per_owner = CLUSTERS // owners
    d_out = lax.dot_general(
        lax.all_gather(out_grad, "head", axis=1, tiled=True),
        w_out,
        (((1,), (1,)), ((), ())),
        preferred_element_type=jnp.float32,
    ).astype(jnp.bfloat16)

    def split_heads(array):
        return array.reshape(frames, heads, HD).transpose(1, 0, 2)

    key_heads = split_heads(keys)
    rows = jnp.concatenate(
        [split_heads(queries), key_heads, split_heads(values), split_heads(d_out)], axis=2
    )
    ids = cluster_ids[:, :, 0]
    member = (ids[:, :, None] == jnp.arange(CLUSTERS, dtype=jnp.int32)[None, None, :]).astype(
        jnp.int32
    )
    running = jnp.cumsum(member, axis=1)
    rank = jnp.sum(member * (running - 1), axis=2)
    slot = ids * MOST + rank
    flat_index = (jnp.arange(heads, dtype=jnp.int32)[:, None] * (CLUSTERS * MOST) + slot).reshape(
        -1
    )
    empty_row = jnp.where(jnp.arange(4 * HD) == 0, EMPTY, 0.0).astype(jnp.bfloat16)
    outgoing = (
        jnp.broadcast_to(empty_row, (heads * CLUSTERS * MOST, 4 * HD))
        .at[flat_index]
        .set(rows.reshape(-1, 4 * HD))
    )
    outgoing = outgoing.reshape(heads, owners, per_owner * MOST, 4 * HD)
    received = lax.all_to_all(outgoing, "seq", split_axis=1, concat_axis=1, tiled=True)
    returned, key_sums = padded_attend(received, per_owner)
    arrived = lax.all_to_all(returned, "seq", split_axis=1, concat_axis=1, tiled=True)
    picked = arrived.reshape(heads * CLUSTERS * MOST, 3 * HD)[flat_index].reshape(
        heads, frames, 3 * HD
    )

    def join_heads(part):
        return part.transpose(1, 0, 2).reshape(frames, heads * HD)

    query_grad = join_heads(picked[:, :, :HD])
    key_grad = join_heads(picked[:, :, HD : 2 * HD])
    value_grad = join_heads(picked[:, :, 2 * HD :])
    centroid_sums = key_sums.transpose(1, 0, 2).reshape(per_owner, heads * HD)
    return (query_grad, key_grad, value_grad, centroid_sums)


def shards(*args):
    *outs, full = two_hop(*args)
    return lax.cond(full[0, 0] > 0, lambda: tuple(padded(*args)), lambda: tuple(outs))


def solution(mesh):
    placed = (
        P("seq", "head"),
        P("seq", "head"),
        P("seq", "head"),
        P("seq", "head"),
        P("head", None),
        P("head", "seq", None),
    )
    return jax.shard_map(
        shards,
        mesh=mesh,
        in_specs=placed,
        out_specs=(P("seq", "head"), P("seq", "head"), P("seq", "head"), P("seq", "head")),
        check_vma=False,
    )
```

time: 110 us -> 101 us (0.918)
  Pallas kernels: 104 us -> 95.9 us
    pallas_call x1, Pallas kernels: 104 us -> 95.9 us  [two_hop(): pl.pallas_call(kernel, name='two_hop', out_shape=(grad, grad, grad, jax.S...]
    unnamed x16 -> x17, local copies, waits for them, and re-layouts: 4.66 us -> 3.26 us
where the time goes in v3:
time: 101 us
  Pallas kernels  95.9 us (95%)
  local copies, waits for them, and re-layouts  3.78 us (4%)
  between operations  1.37 us (1%)
    pallas_call x1, Pallas kernels, two_hop(): pl.pallas_call(kernel, name='two_hop', out_shape=(grad, grad, grad, jax.S...  95.9 us
    unnamed x17, local copies, waits for them, and re-layouts  3.26 us

profile of v3, /device:TPU:1, one launch (start us, length us, event | category | flops | bytes accessed | tf_op | source)
XLA Modules:
  0.0 101.1 jit_solution(12386218673823835976)
XLA Ops:
  0.6 0.7 copy.115
  1.3 0.0 copy-start
  1.3 0.0 copy-start.1
  1.3 0.0 copy-start.2
  1.3 0.0 copy-start.3
  1.3 0.0 copy-start.4
  1.3 95.9 %two_hop.1 = (bf16[256,256]{1,0:T(8,128)(2,1)S(1)}, bf16[256,256]{1,0:T(8,128)(2,1)S(1)}, bf16[256,256]{1,0:T(8,128)(2,1)S(1)}, f32[2,256]{1,0:T(2,128)S(1)}, f32[8,128]{1,0:T(8,128)S(1)}) custom-call(bf16[256,256]{1,0:T(8,128)(2,1)} %q_ref.1, bf16[256,256]{1,0:T(8,128)(2,1)} %k_ref.1, bf16[256,256]{1,0:T(8,128)(2,1)} %v_ref.1, bf16[256,256]{1,0:T(8,128)(2,1)} %og_ref.1, ...), custom_call_target="tpu_custom_call" | custom-call | tf_op jit(solution)/shard_map/two_hop/pallas_call | solution.py:358
  97.3 0.0 copy-start.5
  97.3 0.5 slice.36
  98.4 0.0 copy-done
  98.4 0.0 copy-done.1
  98.5 0.0 copy-done.2
  98.5 0.0 copy-done.3
  98.5 0.0 copy-done.4
  98.5 0.0 copy-done.5
  98.5 0.7 copy.140
  99.2 0.7 copy.141
  99.8 0.7 copy.142
  100.5 0.6 copy.143
  (1 shorter events, 0.0 us)
Async XLA Ops:
  1.3 97.1 %copy-start = (bf16[256,1024]{1,0:T(8,128)(2,1)S(1)}, bf16[256,1024]{1,0:T(8,128)(2,1)}, u32[]{:S(2)}) copy-start(bf16[256,1024]{1,0:T(8,128)(2,1)} %w_ref.1) | copy-start | bytes 1572868
  1.3 97.1 %copy-start.1 = (bf16[256,256]{1,0:T(8,128)(2,1)S(1)}, bf16[256,256]{1,0:T(8,128)(2,1)}, u32[]{:S(2)}) copy-start(bf16[256,256]{1,0:T(8,128)(2,1)} %og_ref.1) | copy-start | bytes 393220
  1.3 97.1 %copy-start.2 = (bf16[256,256]{1,0:T(8,128)(2,1)S(1)}, bf16[256,256]{1,0:T(8,128)(2,1)}, u32[]{:S(2)}) copy-start(bf16[256,256]{1,0:T(8,128)(2,1)} %q_ref.1) | copy-start | bytes 393220
  1.3 97.1 %copy-start.3 = (bf16[256,256]{1,0:T(8,128)(2,1)S(1)}, bf16[256,256]{1,0:T(8,128)(2,1)}, u32[]{:S(2)}) copy-start(bf16[256,256]{1,0:T(8,128)(2,1)} %k_ref.1) | copy-start | bytes 393220
  1.3 97.1 %copy-start.4 = (bf16[256,256]{1,0:T(8,128)(2,1)S(1)}, bf16[256,256]{1,0:T(8,128)(2,1)}, u32[]{:S(2)}) copy-start(bf16[256,256]{1,0:T(8,128)(2,1)} %v_ref.1) | copy-start | bytes 393220
  97.3 1.2 %copy-start.5 = (s32[4,256,1]{1,2,0:T(1,128)S(1)}, s32[4,256,1]{1,2,0:T(1,128)}, u32[]{:S(2)}) copy-start(s32[4,256,1]{1,2,0:T(1,128)} %param.15) | copy-start | bytes 12292

commit v4 on v3

--- a/solution.py
+++ b/solution.py
@@ -19,9 +19,9 @@
 NY = 4
 CAP = 40
 HALF = 24
-ROWS = 2 * CAP
 BACK = CAP + HALF
-NONE = float(ROWS)
+PARTS = ((0, 48), (48, 48), (96, 64))
+ROWS = 160
 
 
 def iota(shape, dim):
@@ -98,38 +98,35 @@
     sub, lane = iota((256, 256), 0), iota((256, 256), 1)
     earlier = onehot(sub < lane)
     ones = jnp.ones((256, 256), BF)
-    group = sub // 16 == lane // 16
-    before = onehot(group & (lane < sub))
-    across = sub // 16 == (lane // 16 + NZ // 2) % NZ
-    upto_pair = onehot(across & ((lane % 16) // 2 <= (sub % 16) // 2))
-    before_pair = onehot(across & ((lane % 16) // 2 < (sub % 16) // 2))
+    before = onehot((sub // 16 == lane // 16) & (lane < sub))
+    across = onehot(sub // 16 == (lane // 16 + NZ // 2) % NZ)
     member, count, zof = [], [], []
     for h in range(4):
-        ids = ids_ref[h : h + 1, :]
+        ids = ids_ref[h]
         row = ((ids >> 2) & 15) * 16 + (ids >> 6) * 4 + (ids & 3)
         zof.append((((row >> 4) + (h % 2) * (NZ // 2)) & (NZ - 1)).astype(F32))
         member.append(onehot(sub == row))
         count.append(nn(member[h], ones).astype(BF))
-    targets = []
+    poses, targets = [], []
     meta = jnp.zeros((8, 128), F32)
     mrow = iota((8, 128), 0)
     for h in range(4):
-        other = nn(before_pair if h % 2 == 0 else upto_pair, count[h ^ 1])
-        place = nn(before, count[h]) + other + nn(member[h], earlier)
+        place = nn(before, count[h]) + nn(member[h], earlier)
+        if h % 2 == 1:
+            place += nn(across, count[h - 1])
         pos = jnp.sum(member[h].astype(F32) * place, axis=0, keepdims=True)
+        poses.append(pos)
         fits = pos < CAP
-        lower = pos < HALF
-        targets.append(jnp.where(fits, zof[h] * CAP + pos, -1.0))
         back = zof[h] * BACK + pos
         targets.append(jnp.where(fits, back, -1.0))
-        targets.append(jnp.where(lower, back + CAP, -1.0))
+        targets.append(jnp.where(pos < HALF, back + CAP, -1.0))
         targets.append(jnp.where(fits & (pos >= HALF), back + CAP - HALF, -1.0))
         held = nt(jnp.ones((8, 256), BF), member[h])
         meta = jnp.where(mrow == 2 * h, held[:, :128], meta)
         meta = jnp.where(mrow == 2 * h + 1, held[:, 128:], meta)
     meta_s[...] = meta.astype(BF)
     meta_r[pl.ds(z, 1)] = meta.astype(BF)[None]
-    tcol[...] = jnp.concatenate(targets + [jnp.zeros((128 - 16, 256), F32)], axis=0).T
+    tcol[...] = jnp.concatenate(targets + [jnp.zeros((128 - 12, 256), F32)], axis=0).T
 
     def beside(a_ref, b, p):
         a = a_ref[:, p * 128 : (p + 1) * 128].astype(F32)
@@ -140,14 +137,20 @@
             jnp.where(low, swap_halves(a), b).astype(BF),
         )
 
-    def pack(pair, p, at):
-        both = jnp.concatenate(pair, axis=0)
-        goal = jnp.concatenate([targets[8 * p], targets[8 * p + 4]], axis=1).astype(jnp.int32)
-        step = 4 * CAP
-        for part in range(4):
-            pick = onehot(iota((step, 512), 0) + part * step == goal)
-            rows = nn(pick, both).reshape(4, CAP, 128).astype(BF)
-            zs[p, part * 4 : part * 4 + 4, at : at + CAP, :] = rows
+    def pack(part, pieces):
+        at, n = PARTS[part]
+        goals, rows = [], []
+        for p, pair, first, last, to in pieces:
+            for i in range(2):
+                pos = poses[2 * p + i]
+                fits = (pos >= first) & (pos < last)
+                goals.append(jnp.where(fits, zof[2 * p + i] * n + pos + to, -1.0))
+                rows.append(pair[i])
+        goals = jnp.concatenate(goals, axis=1).astype(jnp.int32)
+        rows = jnp.concatenate(rows, axis=0)
+        for i in range(4):
+            pick = onehot(iota((4 * n, 1024), 0) + i * 4 * n == goals)
+            zs[i * 4 : i * 4 + 4, at : at + n, :] = nn(pick, rows).astype(BF).reshape(4, n, 128)
 
     pl.semaphore_wait(barrier, NY - 1 + NZ - 1 + NXC - 1)
 
@@ -157,8 +160,8 @@
             device_id=peer, device_id_type=MESH,
         ).start()
 
-    def settle(buf, n, sem, which):
-        part = buf.at[pl.ds(0, n)]
+    def settle(buf, n, sem, which, rows=None):
+        part = buf.at[pl.ds(0, n)] if rows is None else buf.at[pl.ds(0, n), rows]
         pltpu.make_async_copy(part, part, which.at[sem]).wait()
 
     for i in range(1, NY):
@@ -166,29 +169,30 @@
     for i in zorder:
         remote(meta_s, meta_r.at[z], 1, zpeer(i)[1])
 
-    def send_z(src, dst, p, sem):
+    def send_z(src, dst, rows, sem):
         for i in zorder:
             to, peer = zpeer(i)
-            remote(src.at[p, to], dst.at[p, z], sem, peer)
-        own = pltpu.make_async_copy(src.at[p, z], dst.at[p, z], sem_l.at[sem])
-        own.start()
-
-    def wait_z(src, dst, p, sem):
-        settle(dst.at[p], NZ - 1, sem, sem_r)
-        pltpu.make_async_copy(src.at[p, z], dst.at[p, z], sem_l.at[sem]).wait()
-
-    def send_x(src, dst, p, sem):
-        for i in range(1, NXC):
-            to, peer = xpeer(i)
-            remote(src.at[p, to], dst.at[p, xc], sem, peer)
-        pltpu.make_async_copy(src.at[p, xc], dst.at[p, xc], sem_l.at[sem]).start()
-
-    def wait_x(src, dst, p, sem):
-        settle(dst.at[p], NXC - 1, sem, sem_r)
-        pltpu.make_async_copy(src.at[p, xc], dst.at[p, xc], sem_l.at[sem]).wait()
-
-    for p in range(2):
-        pack(beside(q_ref, k_ref, p), p, 0)
+            remote(src.at[to, rows], dst.at[z, rows], sem, peer)
+        pltpu.make_async_copy(src.at[z, rows], dst.at[z, rows], sem_l.at[sem]).start()
+
+    def wait_z(src, dst, rows, sem):
+        settle(dst, NZ - 1, sem, sem_r, rows)
+        pltpu.make_async_copy(src.at[z, rows], dst.at[z, rows], sem_l.at[sem]).wait()
+
+    def send_x(src, dst, p, i, sem):
+        for step in range(1, NXC):
+            to, peer = xpeer(step)
+            remote(src.at[p, i, to], dst.at[p, i, xc], sem, peer)
+        pltpu.make_async_copy(src.at[p, i, xc], dst.at[p, i, xc], sem_l.at[sem]).start()
+
+    def wait_x(src, dst, p, i, sem):
+        settle(dst.at[p, i], NXC - 1, sem, sem_r)
+        pltpu.make_async_copy(src.at[p, i, xc], dst.at[p, i, xc], sem_l.at[sem]).wait()
+
+    rows_of = [pl.ds(at, n) for at, n in PARTS]
+    qk = [beside(q_ref, k_ref, p) for p in range(2)]
+    pack(0, [(0, qk[0], 0, CAP, 0), (1, qk[1], 0, 8, CAP)])
+    send_z(zs, zr, rows_of[0], 2)
     settle(ogr, NY - 1, 0, sem_r)
     grad = jnp.zeros((256, 256), F32)
     for i in range(NY):
@@ -196,25 +200,41 @@
         piece = og_ref[...] if i == 0 else ogr[pl.ds(y, 1)][0]
         grad += nt(piece, w_ref[:, pl.ds(pl.multiple_of(y * 256, 256), 256)])
     d_out = grad.astype(BF)
-    for p in range(2):
-        pack(beside(v_ref, d_out, p), p, CAP)
-        send_z(zs, zr, p, 2 + p)
+    vg = [beside(v_ref, d_out, p) for p in range(2)]
+    pack(1, [(0, vg[0], 0, CAP, 0), (1, qk[1], 8, 16, CAP - 8)])
+    send_z(zs, zr, rows_of[1], 3)
+    pack(2, [(1, qk[1], 16, CAP, -16), (1, vg[1], 0, CAP, CAP - 16)])
+    send_z(zs, zr, rows_of[2], 4)
 
     settle(meta_r, NZ - 1, 1, sem_r)
     r_i, l_i = iota((128, 128), 0), iota((128, 128), 1)
-    slot_row = (l_i // 8) * 2 + (l_i // 2) % 2
-    select = onehot((r_i % 16 == slot_row) & (r_i // 16 == z % 8) & (l_i < 64))
     meta_all = meta_r[...].reshape(128, 128)
-    found = nn(meta_all, select)
-    half = r_i % 2 == (z // 8 + (l_i // 4) % 2) % 2
-    smaller = onehot(r_i < l_i)
+    slot_row = ((l_i // 8) % 8) * 2 + (l_i // 2) % 2
+    found = nn(meta_all, onehot((r_i % 16 == slot_row) & (r_i // 16 == z % 8)))
+    half = r_i % 2 == (z // 8 + l_i // 64) % 2
+
+    def slot(o):
+        return (o // 8) * 4 + o % 4
+
+    smaller = onehot(((r_i // 4) % 2 == 0) & (slot(r_i) < slot(l_i)))
     l16 = iota((16, 128), 1)
+    first_kind = (l16 // 4) % 2 == 0
     for p in range(2):
-        mine = jnp.where(half & ((r_i // 2) % 4 == 2 * p + (l_i // 4) % 2), found, 0.0)
+        mine = jnp.where(half & ((r_i // 2) % 4 == 2 * p + l_i // 64), found, 0.0)
         held = jnp.sum(mine.reshape(16, 8, 128), axis=1)
         taken = held > (l16 % 2).astype(F32)
-        ahead = nn(onehot(taken), smaller)
-        tslot[p] = jnp.where(taken, ahead, NONE)
+        t = nn(onehot(taken), smaller)
+        if p == 0:
+            there, empty = jnp.where(first_kind, t, t + 48), 96.0
+        else:
+            there = jnp.where(first_kind, jnp.where(t < 8, t + 40, t + 80), t + 120)
+            empty = float(ROWS)
+        tslot[p] = jnp.where(taken, there, jnp.where(first_kind, empty, -1.0))
+        fits = taken & (t < CAP)
+        lower = jnp.where(t < HALF, t + CAP, -1.0)
+        upper = jnp.where(t >= HALF, t + CAP - HALF, -1.0)
+        tslot[2 + p] = jnp.where(fits, jnp.where(first_kind, t, lower), -1.0)
+        tslot[4 + p] = jnp.where(fits, jnp.where(first_kind, t, upper), -1.0)
     pair = (l_i // 8 == r_i // 8) & ((l_i % 8) // 4 == (r_i % 8) // 2)
     pair = pair & ((l_i % 2 + (l_i // 2) % 2) % 2 == r_i % 2)
     places = nn(onehot(pair), meta_all).astype(BF)
@@ -224,12 +244,12 @@
     full_xs[...] = full
     full_xr[pl.ds(xc, 1)] = full[None]
     for i in range(1, NXC):
-        remote(full_xs, full_xr.at[xc], 10, xpeer(i)[1])
+        remote(full_xs, full_xr.at[xc], 13, xpeer(i)[1])
 
     s_i, o_i = iota((256, 256), 0), iota((256, 256), 1)
 
     def source(o):
-        return ((o // 2) % 16) * 16 + (o // 128) * 8 + ((o // 32) % 4) * 2 + o % 2
+        return ((o // 32) % 2) * 128 + ((o // 2) % 16) * 8 + (o // 128) * 4 + ((o // 64) % 2) * 2 + o % 2
 
     perm = onehot(o_i == source(s_i))
     perm_back = onehot(s_i == source(o_i))
@@ -237,44 +257,34 @@
     mark = mark.astype(BF)
 
     def expand(p):
-        at = iota((ROWS + 16, 64), 0)
+        n = (96, ROWS)[p]
+        at = iota((n + 16, 128), 0)
         for s in range(NZ):
-            slot = tslot[p, s : s + 1, 0:64].astype(jnp.int32)
-            rows = jnp.concatenate([zr[p, s], mark], axis=0)
-            qk = tn(onehot(at == slot), rows).reshape(8, 8, 128)
-            vg = tn(onehot(at == slot + CAP), rows).reshape(8, 8, 128)
-            xs[p, :, s] = jnp.concatenate([qk, vg], axis=1).astype(BF)
-
-    def work(p):
-        for i in range(NXC):
-            rows = nn(perm, xr[p, i].reshape(256, 128)).astype(BF)
-            for b in range(8):
-                yb[b, i * 32 : (i + 1) * 32, :] = rows[b * 32 : (b + 1) * 32]
-        sums = []
-        for b in range(4):
-            zb[b], zb[4 + b] = cluster_block(yb[b], yb[4 + b])
-            sums.append(jnp.sum(yb[b].astype(F32), axis=0, keepdims=True))
+            pick = onehot(at == tslot[p, s : s + 1, :].astype(jnp.int32))
+            rows = tn(pick, jnp.concatenate([zr[s, 0:n, :], mark], axis=0))
+            xs[p, :, :, s * 8 : s * 8 + 8, :] = rows.reshape(2, 8, 8, 128).astype(BF)
+
+    def work(p, h):
+        for i in range(4):
+            rows = nn(perm, xr[p, h, 2 * i : 2 * i + 2].reshape(256, 128)).astype(BF)
+            for b in range(4):
+                yb[b, i * 64 : (i + 1) * 64, :] = rows[b * 64 : (b + 1) * 64]
         for j in range(2):
-            sum_own[j : j + 1, p * HD : (p + 1) * HD] = sums[j][:, HD:]
-            sum_s[j : j + 1, p * HD : (p + 1) * HD] = sums[2 + j][:, HD:]
-        for i in range(NXC):
-            rows = [zb[b, i * 32 : (i + 1) * 32, :] for b in range(8)]
+            zb[j], zb[2 + j] = cluster_block(yb[j], yb[2 + j])
+            total = jnp.sum(yb[j].astype(F32), axis=0, keepdims=True)
+            (sum_own, sum_s)[h][j : j + 1, p * HD : (p + 1) * HD] = total[:, HD:]
+        for i in range(4):
+            rows = [zb[b, i * 64 : (i + 1) * 64, :] for b in range(4)]
             rows = nn(perm_back, jnp.concatenate(rows, axis=0)).astype(BF)
-            xbs[p, i] = rows.reshape(16, 16, 128)
+            xbs[p, h, 2 * i : 2 * i + 2] = rows.reshape(2, 128, 128)
 
     def compact(p):
         low = iota((BACK, 128), 1) < HD
-        at = iota((BACK, 64), 0)
+        at = iota((BACK, 128), 0)
         for s in range(NZ):
-            slot = tslot[p, s : s + 1, 0:64].astype(jnp.int32)
-            back = xbr[p, :, s].astype(F32)
-            back = [back[:, :8].reshape(64, 128), back[:, 8:].reshape(64, 128)]
-            back = jnp.concatenate(back, axis=0).astype(BF)
-            qk = at == slot
-            lower = (at == slot + CAP) & (slot < HALF)
-            upper = (at + HALF == slot + CAP) & (slot >= HALF) & (slot < CAP)
-            first = nn(jnp.concatenate([onehot(qk), onehot(lower)], axis=1), back)
-            second = nn(jnp.concatenate([onehot(qk), onehot(upper)], axis=1), back)
+            back = xbr[p, :, :, s * 8 : s * 8 + 8, :].reshape(128, 128)
+            first = nn(onehot(at == tslot[2 + p, s : s + 1, :].astype(jnp.int32)), back)
+            second = nn(onehot(at == tslot[4 + p, s : s + 1, :].astype(jnp.int32)), back)
             zbs[p, s] = jnp.where(low, first, second).astype(BF)
 
     def unpack(p):
@@ -282,68 +292,80 @@
         rows = zbr[p].reshape(NZ * BACK, 128)
         at = iota((256, NZ * BACK), 1)
         for h in (2 * p, 2 * p + 1):
-            cols = tcol[:, 4 * h : 4 * h + 4].astype(jnp.int32)
-            got = nn(onehot(at == cols[:, 1:2]), rows)
-            first = nn(onehot(at == cols[:, 2:3]), rows)
-            second = nn(onehot(at == cols[:, 3:4]), rows)
+            cols = tcol[:, 3 * h : 3 * h + 3].astype(jnp.int32)
+            got = nn(onehot(at == cols[:, 0:1]), rows)
+            first = nn(onehot(at == cols[:, 1:2]), rows)
+            second = nn(onehot(at == cols[:, 2:3]), rows)
             keys.append(got[:, :HD])
             queries.append(got[:, HD:])
             values.append(first[:, :HD] + second[:, HD:])
         for ref, parts in ((dq_ref, queries), (dk_ref, keys), (dv_ref, values)):
             ref[:, p * 128 : (p + 1) * 128] = jnp.concatenate(parts, axis=1).astype(BF)
 
+    every = pl.ds(0, BACK)
+
+    def forward(p):
+        expand(p)
+        for h in range(2):
+            send_x(xs, xr, p, h, 5 + 2 * p + h)
+
+    def middle(p, h):
+        wait_x(xs, xr, p, h, 5 + 2 * p + h)
+        work(p, h)
+        send_x(xbs, xbr, p, h, 9 + 2 * p + h)
+
     def send_back(p):
-        wait_x(xbs, xbr, p, 6 + p)
+        for h in range(2):
+            wait_x(xbs, xbr, p, h, 9 + 2 * p + h)
         compact(p)
-        send_z(zbs, zbr, p, 8 + p)
-
-    wait_z(zs, zr, 0, 2)
-    expand(0)
-    send_x(xs, xr, 0, 4)
-    settle(full_xr, NXC - 1, 10, sem_r)
+        send_z(zbs.at[p], zbr.at[p], every, 14 + p)
+
+    wait_z(zs, zr, rows_of[0], 2)
+    wait_z(zs, zr, rows_of[1], 3)
+    forward(0)
+    settle(full_xr, NXC - 1, 13, sem_r)
     full = jnp.max(full_xr[...], axis=0)
     full_ys[...] = full
     for i in range(1, NY):
-        remote(full_ys, full_yr.at[hd], 11, ypeer(i))
-    wait_x(xs, xr, 0, 4)
-    work(0)
-    send_x(xbs, xbr, 0, 6)
-    wait_z(zs, zr, 1, 3)
-    expand(1)
-    send_x(xs, xr, 1, 5)
+        remote(full_ys, full_yr.at[hd], 16, ypeer(i))
+    middle(0, 0)
+    middle(0, 1)
+    wait_z(zs, zr, rows_of[2], 4)
+    forward(1)
     send_back(0)
-    wait_x(xs, xr, 1, 5)
-    work(1)
-    send_x(xbs, xbr, 1, 7)
-    remote(sum_s, sum_r, 12, zpeer(NZ // 2)[1])
+    middle(1, 0)
+    middle(1, 1)
+    remote(sum_s, sum_r, 17, zpeer(NZ // 2)[1])
     send_back(1)
-    pltpu.make_async_copy(sum_r, sum_r, sem_r.at[12]).wait()
+    pltpu.make_async_copy(sum_r, sum_r, sem_r.at[17]).wait()
     for p in range(2):
         cols = slice(p * HD, (p + 1) * HD)
         cs_ref[:, p * 128 : (p + 1) * 128] = jnp.concatenate(
             [sum_own[0:2, cols], sum_r[0:2, cols]], axis=1
         )
-    settle(full_yr, NY - 1, 11, sem_r)
+    settle(full_yr, NY - 1, 16, sem_r)
     for i in range(1, NY):
         full = jnp.maximum(full, full_yr[pl.ds((hd + i) % NY, 1)][0])
     full_ref[...] = full
     for p in range(2):
-        wait_z(zbs, zbr, p, 8 + p)
+        wait_z(zbs.at[p], zbr.at[p], every, 14 + p)
         unpack(p)
 
     for i in range(1, NY):
         pltpu.make_async_copy(og_ref, og_ref, sem_s.at[0]).wait()
-        pltpu.make_async_copy(full_ys, full_ys, sem_s.at[11]).wait()
+        pltpu.make_async_copy(full_ys, full_ys, sem_s.at[16]).wait()
     for i in range(1, NZ):
         pltpu.make_async_copy(meta_s, meta_s, sem_s.at[1]).wait()
     for i in range(1, NXC):
-        pltpu.make_async_copy(full_xs, full_xs, sem_s.at[10]).wait()
-    pltpu.make_async_copy(sum_s, sum_s, sem_s.at[12]).wait()
+        pltpu.make_async_copy(full_xs, full_xs, sem_s.at[13]).wait()
+    pltpu.make_async_copy(sum_s, sum_s, sem_s.at[17]).wait()
+    for i in range(3):
+        settle(zs, NZ - 1, 2 + i, sem_s, rows_of[i])
     for p in range(2):
-        settle(zs.at[p], NZ - 1, 2 + p, sem_s)
-        settle(xs.at[p], NXC - 1, 4 + p, sem_s)
-        settle(xbs.at[p], NXC - 1, 6 + p, sem_s)
-        settle(zbs.at[p], NZ - 1, 8 + p, sem_s)
+        for h in range(2):
+            settle(xs.at[p, h], NXC - 1, 5 + 2 * p + h, sem_s)
+            settle(xbs.at[p, h], NXC - 1, 9 + 2 * p + h, sem_s)
+        settle(zbs.at[p], NZ - 1, 14 + p, sem_s)
 
 
 def two_hop(queries, keys, values, out_grad, w_out, cluster_ids):
@@ -368,18 +390,18 @@
             buf(NY, frames, width),
             buf(8, 128),
             buf(NZ, 8, 128),
-            buf(2, NZ, ROWS, 128),
-            buf(2, NZ, ROWS, 128),
-            buf(2, NXC, NZ, 16, 128),
-            buf(2, NXC, NZ, 16, 128),
-            buf(8, 256, 128),
-            buf(8, 256, 128),
-            buf(2, NXC, NZ, 16, 128),
-            buf(2, NXC, NZ, 16, 128),
+            buf(NZ, ROWS, 128),
+            buf(NZ, ROWS, 128),
+            buf(2, 2, NXC, NZ * 8, 128),
+            buf(2, 2, NXC, NZ * 8, 128),
+            buf(4, 256, 128),
+            buf(4, 256, 128),
+            buf(2, 2, NXC, NZ * 8, 128),
+            buf(2, 2, NXC, NZ * 8, 128),
             buf(2, NZ, BACK, 128),
             buf(2, NZ, BACK, 128),
             buf(256, 128, dtype=F32),
-            buf(2, NZ, 128, dtype=F32),
+            buf(6, NZ, 128, dtype=F32),
             buf(8, 128, dtype=F32),
             buf(8, 128, dtype=F32),
             buf(8, 128, dtype=F32),
@@ -387,14 +409,14 @@
             buf(NXC, 8, 128, dtype=F32),
             buf(8, 128, dtype=F32),
             buf(NY, 8, 128, dtype=F32),
-            pltpu.SemaphoreType.DMA((13,)),
-            pltpu.SemaphoreType.DMA((13,)),
-            pltpu.SemaphoreType.DMA((13,)),
+            pltpu.SemaphoreType.DMA((18,)),
+            pltpu.SemaphoreType.DMA((18,)),
+            pltpu.SemaphoreType.DMA((18,)),
         ],
         compiler_params=pltpu.CompilerParams(
             collective_id=0, has_side_effects=True, vmem_limit_bytes=48 << 20
         ),
-    )(queries, keys, values, out_grad, w_out, cluster_ids.reshape(heads, frames))
+    )(queries, keys, values, out_grad, w_out, cluster_ids.reshape(heads, 1, frames))
 
 
 def padded_block(block, live):

time: 101 us -> 89.5 us (0.89)
  Pallas kernels: 95.9 us -> 84.7 us
    pallas_call x1, Pallas kernels: 95.9 us -> 84.7 us  [two_hop(): pl.pallas_call(kernel, name='two_hop', out_shape=(grad, grad, grad, jax.S...]
    unnamed x17 -> x16, local copies, waits for them, and re-layouts: 3.26 us -> 2.57 us
where the time goes in v4:
time: 89.5 us; the launch traced here: 89.4 us
  Pallas kernels  84.7 us (95%)
  local copies, waits for them, and re-layouts  3.09 us (3%)
  between operations  1.4 us (2%)
    pallas_call x1, Pallas kernels, two_hop(): pl.pallas_call(kernel, name='two_hop', out_shape=(grad, grad, grad, jax.S...  84.7 us
    unnamed x16, local copies, waits for them, and re-layouts  2.57 us

profile of v4, /device:TPU:1, one launch (start us, length us, event | category | flops | bytes accessed | tf_op | source)
XLA Modules:
  0.0 89.4 jit_solution(3242784193103265939)
XLA Ops:
  0.6 0.0 copy-start
  0.6 0.0 copy-start.1
  0.7 0.0 copy-start.2
  0.7 0.0 copy-start.3
  0.7 0.0 copy-start.4
  0.7 84.7 %two_hop.1 = (bf16[256,256]{1,0:T(8,128)(2,1)S(1)}, bf16[256,256]{1,0:T(8,128)(2,1)S(1)}, bf16[256,256]{1,0:T(8,128)(2,1)S(1)}, f32[2,256]{1,0:T(2,128)S(1)}, f32[8,128]{1,0:T(8,128)S(1)}) custom-call(bf16[256,256]{1,0:T(8,128)(2,1)} %q_ref.1, bf16[256,256]{1,0:T(8,128)(2,1)} %k_ref.1, bf16[256,256]{1,0:T(8,128)(2,1)} %v_ref.1, bf16[256,256]{1,0:T(8,128)(2,1)} %og_ref.1, ...), custom_call_target="tpu_custom_call" | custom-call | tf_op jit(solution)/shard_map/two_hop/pallas_call | solution.py:380
  85.4 0.0 copy-start.5
  85.4 0.5 slice.36
  86.5 0.0 copy-done
  86.6 0.0 copy-done.1
  86.6 0.0 copy-done.2
  86.6 0.0 copy-done.3
  86.6 0.0 copy-done.4
  86.6 0.0 copy-done.5
  86.6 0.2 conditional.1
  86.8 0.7 copy.137
  87.5 0.7 copy.138
  88.2 0.7 copy.139
  88.8 0.6 copy.140
Async XLA Ops:
  0.6 85.9 %copy-start = (bf16[256,1024]{1,0:T(8,128)(2,1)S(1)}, bf16[256,1024]{1,0:T(8,128)(2,1)}, u32[]{:S(2)}) copy-start(bf16[256,1024]{1,0:T(8,128)(2,1)} %w_ref.1) | copy-start | bytes 1572868
  0.6 85.9 %copy-start.1 = (bf16[256,256]{1,0:T(8,128)(2,1)S(1)}, bf16[256,256]{1,0:T(8,128)(2,1)}, u32[]{:S(2)}) copy-start(bf16[256,256]{1,0:T(8,128)(2,1)} %og_ref.1) | copy-start | bytes 393220
  0.7 85.9 %copy-start.2 = (bf16[256,256]{1,0:T(8,128)(2,1)S(1)}, bf16[256,256]{1,0:T(8,128)(2,1)}, u32[]{:S(2)}) copy-start(bf16[256,256]{1,0:T(8,128)(2,1)} %q_ref.1) | copy-start | bytes 393220
  0.7 85.9 %copy-start.3 = (bf16[256,256]{1,0:T(8,128)(2,1)S(1)}, bf16[256,256]{1,0:T(8,128)(2,1)}, u32[]{:S(2)}) copy-start(bf16[256,256]{1,0:T(8,128)(2,1)} %k_ref.1) | copy-start | bytes 393220
  0.7 85.9 %copy-start.4 = (bf16[256,256]{1,0:T(8,128)(2,1)S(1)}, bf16[256,256]{1,0:T(8,128)(2,1)}, u32[]{:S(2)}) copy-start(bf16[256,256]{1,0:T(8,128)(2,1)} %v_ref.1) | copy-start | bytes 393220
  85.4 1.2 %copy-start.5 = (s32[4,256,1]{1,2,0:T(1,128)S(1)}, s32[4,256,1]{1,2,0:T(1,128)}, u32[]{:S(2)}) copy-start(s32[4,256,1]{1,2,0:T(1,128)} %param.15) | copy-start | bytes 12292

commit v5 on v4

--- a/solution.py
+++ b/solution.py
@@ -18,6 +18,8 @@
 NXC = 8
 NY = 4
 CAP = 40
+CAP_HEAD = 24
+HEAD0 = CAP - CAP_HEAD
 HALF = 24
 BACK = CAP + HALF
 PARTS = ((0, 48), (48, 48), (96, 64))
@@ -66,12 +68,34 @@
     return jnp.where(low, dk, dq).astype(BF), jnp.where(low, swap_halves(dv), dv).astype(BF)
 
 
+def unpack(p, rows, tcol):
+    keys, values, queries = [], [], []
+    at = iota((256, NZ * BACK), 1)
+    for h in (2 * p, 2 * p + 1):
+        cols = tcol[:, 3 * h : 3 * h + 3].astype(jnp.int32)
+        got = nn(onehot(at == cols[:, 0:1]), rows)
+        first = nn(onehot(at == cols[:, 1:2]), rows)
+        second = nn(onehot(at == cols[:, 2:3]), rows)
+        keys.append(got[:, :HD])
+        queries.append(got[:, HD:])
+        values.append(first[:, :HD] + second[:, HD:])
+    return [jnp.concatenate(x, axis=1).astype(BF) for x in (queries, keys, values)]
+
+
+def last_kernel(done_ref, rest_ref, tcol, cs_in, dq_ref, dk_ref, dv_ref, cs_ref):
+    cs_ref[...] = cs_in[...]
+    parts = unpack(1, rest_ref[...], tcol)
+    for i, ref in enumerate((dq_ref, dk_ref, dv_ref)):
+        ref[:, 0:128] = done_ref[i]
+        ref[:, 128:256] = parts[i]
+
+
 def kernel(
-    q_ref, k_ref, v_ref, og_ref, w_ref, ids_ref,
-    dq_ref, dk_ref, dv_ref, cs_ref, full_ref,
-    ogr, meta_s, meta_r, zs, zr, xs, xr, yb, zb, xbs, xbr, zbs, zbr, tcol, tslot,
+    q_hbm, k_hbm, v_hbm, og_hbm, w_hbm, ids_hbm,
+    done_ref, rest_ref, tcol, cs_ref, full_ref,
+    q_ref, k_ref, v_ref, og_ref, w_ref, ids_ref, ogr, meta_s, meta_r, zs, zr, xs, xr, yb, zb, xbs, xbr, zbs, zbr, tslot,
     sum_own, sum_s, sum_r, full_xs, full_xr, full_ys, full_yr,
-    sem_s, sem_r, sem_l,
+    sem_s, sem_r, sem_l, sem_in,
 ):
     me, hd = lax.axis_index("seq"), lax.axis_index("head")
     x, z, c = me // (2 * NZ), (me // 2) % NZ, me % 2
@@ -95,11 +119,21 @@
     for peer in peers:
         pl.semaphore_signal(barrier, inc=1, device_id=peer, device_id_type=MESH)
 
+    loads = [
+        pltpu.make_async_copy(src, dst, sem_in.at[i])
+        for i, (src, dst) in enumerate(
+            ((ids_hbm, ids_ref), (q_hbm, q_ref), (k_hbm, k_ref),
+             (og_hbm, og_ref), (v_hbm, v_ref), (w_hbm, w_ref))
+        )
+    ]
+    for load in loads:
+        load.start()
+    loads[0].wait()
+
     sub, lane = iota((256, 256), 0), iota((256, 256), 1)
     earlier = onehot(sub < lane)
     ones = jnp.ones((256, 256), BF)
     before = onehot((sub // 16 == lane // 16) & (lane < sub))
-    across = onehot(sub // 16 == (lane // 16 + NZ // 2) % NZ)
     member, count, zof = [], [], []
     for h in range(4):
         ids = ids_ref[h]
@@ -112,14 +146,13 @@
     mrow = iota((8, 128), 0)
     for h in range(4):
         place = nn(before, count[h]) + nn(member[h], earlier)
-        if h % 2 == 1:
-            place += nn(across, count[h - 1])
-        pos = jnp.sum(member[h].astype(F32) * place, axis=0, keepdims=True)
-        poses.append(pos)
-        fits = pos < CAP
+        nth = jnp.sum(member[h].astype(F32) * place, axis=0, keepdims=True)
+        fits = nth < CAP_HEAD
+        pos = nth if h % 2 == 0 else CAP - 1 - nth
+        poses.append(jnp.where(fits, pos, -1.0))
         back = zof[h] * BACK + pos
         targets.append(jnp.where(fits, back, -1.0))
-        targets.append(jnp.where(pos < HALF, back + CAP, -1.0))
+        targets.append(jnp.where(fits & (pos < HALF), back + CAP, -1.0))
         targets.append(jnp.where(fits & (pos >= HALF), back + CAP - HALF, -1.0))
         held = nt(jnp.ones((8, 256), BF), member[h])
         meta = jnp.where(mrow == 2 * h, held[:, :128], meta)
@@ -165,7 +198,7 @@
         pltpu.make_async_copy(part, part, which.at[sem]).wait()
 
     for i in range(1, NY):
-        remote(og_ref, ogr.at[hd], 0, ypeer(i))
+        remote(og_hbm, ogr.at[hd], 0, ypeer(i))
     for i in zorder:
         remote(meta_s, meta_r.at[z], 1, zpeer(i)[1])
 
@@ -190,9 +223,13 @@
         pltpu.make_async_copy(src.at[p, i, xc], dst.at[p, i, xc], sem_l.at[sem]).wait()
 
     rows_of = [pl.ds(at, n) for at, n in PARTS]
+    loads[1].wait()
+    loads[2].wait()
     qk = [beside(q_ref, k_ref, p) for p in range(2)]
     pack(0, [(0, qk[0], 0, CAP, 0), (1, qk[1], 0, 8, CAP)])
     send_z(zs, zr, rows_of[0], 2)
+    for load in loads[3:]:
+        load.wait()
     settle(ogr, NY - 1, 0, sem_r)
     grad = jnp.zeros((256, 256), F32)
     for i in range(NY):
@@ -216,7 +253,8 @@
     def slot(o):
         return (o // 8) * 4 + o % 4
 
-    smaller = onehot(((r_i // 4) % 2 == 0) & (slot(r_i) < slot(l_i)))
+    smaller = ((r_i // 4) % 2 == 0) & (slot(r_i) < slot(l_i))
+    smaller = onehot(smaller & (r_i // 64 == l_i // 64))
     l16 = iota((16, 128), 1)
     first_kind = (l16 // 4) % 2 == 0
     for p in range(2):
@@ -224,13 +262,15 @@
         held = jnp.sum(mine.reshape(16, 8, 128), axis=1)
         taken = held > (l16 % 2).astype(F32)
         t = nn(onehot(taken), smaller)
+        fits = taken & (t < CAP_HEAD)
+        t = jnp.where(l16 < 64, t, CAP - 1 - t)
         if p == 0:
             there, empty = jnp.where(first_kind, t, t + 48), 96.0
         else:
             there = jnp.where(first_kind, jnp.where(t < 8, t + 40, t + 80), t + 120)
             empty = float(ROWS)
+        there = jnp.where(fits, there, -1.0)
         tslot[p] = jnp.where(taken, there, jnp.where(first_kind, empty, -1.0))
-        fits = taken & (t < CAP)
         lower = jnp.where(t < HALF, t + CAP, -1.0)
         upper = jnp.where(t >= HALF, t + CAP - HALF, -1.0)
         tslot[2 + p] = jnp.where(fits, jnp.where(first_kind, t, lower), -1.0)
@@ -238,9 +278,10 @@
     pair = (l_i // 8 == r_i // 8) & ((l_i % 8) // 4 == (r_i % 8) // 2)
     pair = pair & ((l_i % 2 + (l_i // 2) % 2) % 2 == r_i % 2)
     places = nn(onehot(pair), meta_all).astype(BF)
-    places = nn(places, onehot(r_i // 16 == l_i))
-    most = jnp.max(jnp.max(places, axis=0, keepdims=True), axis=1, keepdims=True)
-    full = jnp.broadcast_to(jnp.where(most > CAP, 1.0, 0.0), (8, 128))
+    blocks = onehot(r_i // 16 == l_i)
+    over = (nn(places, blocks) > CAP) | (nn(meta_all, blocks) > CAP_HEAD)
+    over = jnp.max(jnp.where(over, 1.0, 0.0), axis=0, keepdims=True)
+    full = jnp.broadcast_to(jnp.max(over, axis=1, keepdims=True), (8, 128))
     full_xs[...] = full
     full_xr[pl.ds(xc, 1)] = full[None]
     for i in range(1, NXC):
@@ -278,31 +319,23 @@
             rows = nn(perm_back, jnp.concatenate(rows, axis=0)).astype(BF)
             xbs[p, h, 2 * i : 2 * i + 2] = rows.reshape(2, 128, 128)
 
-    def compact(p):
-        low = iota((BACK, 128), 1) < HD
-        at = iota((BACK, 128), 0)
+    def compact_head0(p):
+        at = iota((HEAD0, 64), 0)
+        for s in range(NZ):
+            back = xbr[p, 0, :, s * 8 : s * 8 + 8, :].reshape(64, 128)
+            pick = at == tslot[2 + p, s : s + 1, 0:64].astype(jnp.int32)
+            zbs[p, s, 0:HEAD0, :] = nn(onehot(pick), back).astype(BF)
+
+    def compact_rest(p):
+        low = iota((BACK - HEAD0, 128), 1) < HD
+        at = iota((BACK - HEAD0, 128), 0) + HEAD0
         for s in range(NZ):
             back = xbr[p, :, :, s * 8 : s * 8 + 8, :].reshape(128, 128)
             first = nn(onehot(at == tslot[2 + p, s : s + 1, :].astype(jnp.int32)), back)
             second = nn(onehot(at == tslot[4 + p, s : s + 1, :].astype(jnp.int32)), back)
-            zbs[p, s] = jnp.where(low, first, second).astype(BF)
-
-    def unpack(p):
-        keys, values, queries = [], [], []
-        rows = zbr[p].reshape(NZ * BACK, 128)
-        at = iota((256, NZ * BACK), 1)
-        for h in (2 * p, 2 * p + 1):
-            cols = tcol[:, 3 * h : 3 * h + 3].astype(jnp.int32)
-            got = nn(onehot(at == cols[:, 0:1]), rows)
-            first = nn(onehot(at == cols[:, 1:2]), rows)
-            second = nn(onehot(at == cols[:, 2:3]), rows)
-            keys.append(got[:, :HD])
-            queries.append(got[:, HD:])
-            values.append(first[:, :HD] + second[:, HD:])
-        for ref, parts in ((dq_ref, queries), (dk_ref, keys), (dv_ref, values)):
-            ref[:, p * 128 : (p + 1) * 128] = jnp.concatenate(parts, axis=1).astype(BF)
-
-    every = pl.ds(0, BACK)
+            zbs[p, s, HEAD0:BACK, :] = jnp.where(low, first, second).astype(BF)
+
+    head0, rest = pl.ds(0, HEAD0), pl.ds(HEAD0, BACK - HEAD0)
 
     def forward(p):
         expand(p)
@@ -315,10 +348,16 @@
         send_x(xbs, xbr, p, h, 9 + 2 * p + h)
 
     def send_back(p):
-        for h in range(2):
-            wait_x(xbs, xbr, p, h, 9 + 2 * p + h)
-        compact(p)
-        send_z(zbs.at[p], zbr.at[p], every, 14 + p)
+        wait_x(xbs, xbr, p, 0, 9 + 2 * p)
+        compact_head0(p)
+        send_z(zbs.at[p], zbr.at[p], head0, 14 + 2 * p)
+        wait_x(xbs, xbr, p, 1, 10 + 2 * p)
+        compact_rest(p)
+        send_z(zbs.at[p], zbr.at[p], rest, 15 + 2 * p)
+
+    def wait_back(p):
+        wait_z(zbs.at[p], zbr.at[p], head0, 14 + 2 * p)
+        wait_z(zbs.at[p], zbr.at[p], rest, 15 + 2 * p)
 
     wait_z(zs, zr, rows_of[0], 2)
     wait_z(zs, zr, rows_of[1], 3)
@@ -327,7 +366,7 @@
     full = jnp.max(full_xr[...], axis=0)
     full_ys[...] = full
     for i in range(1, NY):
-        remote(full_ys, full_yr.at[hd], 16, ypeer(i))
+        remote(full_ys, full_yr.at[hd], 18, ypeer(i))
     middle(0, 0)
     middle(0, 1)
     wait_z(zs, zr, rows_of[2], 4)
@@ -335,44 +374,46 @@
     send_back(0)
     middle(1, 0)
     middle(1, 1)
-    remote(sum_s, sum_r, 17, zpeer(NZ // 2)[1])
+    remote(sum_s, sum_r, 19, zpeer(NZ // 2)[1])
     send_back(1)
-    pltpu.make_async_copy(sum_r, sum_r, sem_r.at[17]).wait()
+    pltpu.make_async_copy(sum_r, sum_r, sem_r.at[19]).wait()
     for p in range(2):
         cols = slice(p * HD, (p + 1) * HD)
         cs_ref[:, p * 128 : (p + 1) * 128] = jnp.concatenate(
             [sum_own[0:2, cols], sum_r[0:2, cols]], axis=1
         )
-    settle(full_yr, NY - 1, 16, sem_r)
+    settle(full_yr, NY - 1, 18, sem_r)
     for i in range(1, NY):
         full = jnp.maximum(full, full_yr[pl.ds((hd + i) % NY, 1)][0])
-    full_ref[...] = full
-    for p in range(2):
-        wait_z(zbs.at[p], zbr.at[p], every, 14 + p)
-        unpack(p)
+    full_ref[0, 0] = jnp.max(full).astype(jnp.int32)
+    wait_back(0)
+    for i, part in enumerate(unpack(0, zbr[0].reshape(NZ * BACK, 128), tcol)):
+        done_ref[i] = part
+    wait_back(1)
+    rest_ref[...] = zbr[1].reshape(NZ * BACK, 128)
 
     for i in range(1, NY):
         pltpu.make_async_copy(og_ref, og_ref, sem_s.at[0]).wait()
-        pltpu.make_async_copy(full_ys, full_ys, sem_s.at[16]).wait()
+        pltpu.make_async_copy(full_ys, full_ys, sem_s.at[18]).wait()
     for i in range(1, NZ):
         pltpu.make_async_copy(meta_s, meta_s, sem_s.at[1]).wait()
     for i in range(1, NXC):
         pltpu.make_async_copy(full_xs, full_xs, sem_s.at[13]).wait()
-    pltpu.make_async_copy(sum_s, sum_s, sem_s.at[17]).wait()
+    pltpu.make_async_copy(sum_s, sum_s, sem_s.at[19]).wait()
     for i in range(3):
         settle(zs, NZ - 1, 2 + i, sem_s, rows_of[i])
     for p in range(2):
         for h in range(2):
             settle(xs.at[p, h], NXC - 1, 5 + 2 * p + h, sem_s)
             settle(xbs.at[p, h], NXC - 1, 9 + 2 * p + h, sem_s)
-        settle(zbs.at[p], NZ - 1, 14 + p, sem_s)
+        settle(zbs.at[p], NZ - 1, 14 + 2 * p, sem_s, head0)
+        settle(zbs.at[p], NZ - 1, 15 + 2 * p, sem_s, rest)
 
 
 def two_hop(queries, keys, values, out_grad, w_out, cluster_ids):
     frames, width = queries.shape
     heads = cluster_ids.shape[0]
     vmem = pl.BlockSpec(memory_space=pltpu.VMEM)
-    grad = jax.ShapeDtypeStruct((frames, width), BF)
 
     def buf(*shape, dtype=BF):
         return pltpu.VMEM(shape, dtype)
@@ -381,12 +422,21 @@
         kernel,
         name="two_hop",
         out_shape=(
-            grad, grad, grad,
-            jax.ShapeDtypeStruct((2, width), F32), jax.ShapeDtypeStruct((8, 128), F32),
+            jax.ShapeDtypeStruct((3, frames, width // 2), BF),
+            jax.ShapeDtypeStruct((NZ * BACK, 128), BF),
+            jax.ShapeDtypeStruct((frames, 128), F32),
+            jax.ShapeDtypeStruct((2, width), F32),
+            jax.ShapeDtypeStruct((1, 1), jnp.int32),
         ),
-        in_specs=[vmem] * 6,
-        out_specs=(vmem,) * 5,
+        in_specs=[pl.BlockSpec(memory_space=pl.ANY)] * 6,
+        out_specs=(vmem,) * 4 + (pl.BlockSpec(memory_space=pltpu.SMEM),),
         scratch_shapes=[
+            buf(frames, width),
+            buf(frames, width),
+            buf(frames, width),
+            buf(frames, width),
+            buf(width, NY * width),
+            buf(heads, 1, frames, dtype=jnp.int32),
             buf(NY, frames, width),
             buf(8, 128),
             buf(NZ, 8, 128),
@@ -400,7 +450,6 @@
             buf(2, 2, NXC, NZ * 8, 128),
             buf(2, NZ, BACK, 128),
             buf(2, NZ, BACK, 128),
-            buf(256, 128, dtype=F32),
             buf(6, NZ, 128, dtype=F32),
             buf(8, 128, dtype=F32),
             buf(8, 128, dtype=F32),
@@ -409,9 +458,10 @@
             buf(NXC, 8, 128, dtype=F32),
             buf(8, 128, dtype=F32),
             buf(NY, 8, 128, dtype=F32),
-            pltpu.SemaphoreType.DMA((18,)),
-            pltpu.SemaphoreType.DMA((18,)),
-            pltpu.SemaphoreType.DMA((18,)),
+            pltpu.SemaphoreType.DMA((20,)),
+            pltpu.SemaphoreType.DMA((20,)),
+            pltpu.SemaphoreType.DMA((20,)),
+            pltpu.SemaphoreType.DMA((6,)),
         ],
         compiler_params=pltpu.CompilerParams(
             collective_id=0, has_side_effects=True, vmem_limit_bytes=48 << 20
@@ -513,9 +563,36 @@
     return (query_grad, key_grad, value_grad, centroid_sums)
 
 
+def last_step(done, rest, tcol, sums):
+    frames, width = done.shape[1], 2 * done.shape[2]
+    vmem = pl.BlockSpec(memory_space=pltpu.VMEM)
+    grad = jax.ShapeDtypeStruct((frames, width), BF)
+    return pl.pallas_call(
+        last_kernel,
+        name="last_step",
+        out_shape=(grad, grad, grad, jax.ShapeDtypeStruct(sums.shape, F32)),
+        in_specs=[vmem] * 4,
+        out_specs=(vmem,) * 4,
+        compiler_params=pltpu.CompilerParams(vmem_limit_bytes=16 << 20),
+    )(done, rest, tcol, sums)
+
+
+def as_parts(dq, dk, dv, sums):
+    frames = dq.shape[0]
+    done = jnp.stack([x[:, :128] for x in (dq, dk, dv)])
+    rest = [jnp.concatenate([dk[:, at : at + HD], dq[:, at : at + HD]], axis=1) for at in (128, 192)]
+    rest = jnp.concatenate(rest + [dv[:, 128:], jnp.zeros((NZ * BACK - 3 * frames, 128), BF)])
+    at = jnp.arange(frames, dtype=F32)[:, None]
+    none = jnp.full((frames, 1), -1.0, F32)
+    second = [at, at + 2 * frames, none, at + frames, none, at + 2 * frames]
+    cols = [jnp.zeros((frames, 6), F32)] + second + [jnp.zeros((frames, 116), F32)]
+    return done, rest, jnp.concatenate(cols, axis=1), sums
+
+
 def shards(*args):
-    *outs, full = two_hop(*args)
-    return lax.cond(full[0, 0] > 0, lambda: tuple(padded(*args)), lambda: tuple(outs))
+    *parts, full = two_hop(*args)
+    parts = lax.cond(full[0, 0] > 0, lambda: as_parts(*padded(*args)), lambda: tuple(parts))
+    return tuple(last_step(*parts))
 
 
 def solution(mesh):

time: 89.5 us -> 85.3 us (0.953)
  local copies, waits for them, and re-layouts: 3.09 us -> 0.03 us
  Pallas kernels: 84.7 us -> 83.4 us
    unnamed x16 -> x12, local copies, waits for them, and re-layouts: 2.57 us -> 0.03 us
    pallas_call x1 -> x2, Pallas kernels: 84.7 us -> 83.4 us  [the longest x1 81.5 us: two_hop(): pl.pallas_call(kernel, name='two_hop', out_shape=(jax.ShapeDtypeStruct((3...]
where the time goes in v5:
time: 85.3 us; the launch traced here: 85.1 us
  Pallas kernels  83.4 us (98%)
  between operations  1.45 us (2%)
    pallas_call x1, Pallas kernels, two_hop(): pl.pallas_call(kernel, name='two_hop', out_shape=(jax.ShapeDtypeStruct((3...  81.5 us
    pallas_call x1, Pallas kernels, last_step(): pl.pallas_call(last_kernel, name='last_step', out_shape=(grad, grad, grad...  1.88 us

profile of v5, /device:TPU:1, one launch (start us, length us, event | category | flops | bytes accessed | tf_op | source)
XLA Modules:
  0.0 85.1 jit_solution(17529736345178041740)
XLA Ops:
  0.6 0.0 copy-start
  0.6 0.0 copy-start.1
  0.7 0.0 copy-start.2
  0.7 0.0 copy-start.3
  0.7 0.0 copy-start.4
  0.7 81.5 %two_hop.1 = (bf16[3,256,128]{2,1,0:T(8,128)(2,1)S(1)}, bf16[1024,128]{1,0:T(8,128)(2,1)S(1)}, f32[256,128]{1,0:T(8,128)S(1)}, f32[2,256]{1,0:T(2,128)S(1)}, s32[1,1]{1,0:T(1,128)}) custom-call(bf16[256,256]{1,0:T(8,128)(2,1)} %q_hbm.1, bf16[256,256]{1,0:T(8,128)(2,1)} %k_hbm.1, bf16[256,256]{1,0:T(8,128)(2,1)} %v_hbm.1, bf16[256,256]{1,0:T(8,128)(2,1)} %og_hbm.1, ...), custom_call_target="tpu_custom_call" | custom-call | tf_op jit(solution)/shard_map/two_hop/pallas_call | solution.py:421
  82.2 0.0 copy-start.6
  82.9 0.0 copy-done
  82.9 0.0 copy-done.1
  82.9 0.0 copy-done.2
  82.9 0.0 copy-done.3
  83.0 0.0 copy-done.4
  83.0 0.0 copy-done.6
  83.0 0.2 conditional.1
  83.2 1.9 %last_step.1 = (bf16[256,256]{1,0:T(8,128)(2,1)}, bf16[256,256]{1,0:T(8,128)(2,1)}, bf16[256,256]{1,0:T(8,128)(2,1)}, f32[2,256]{1,0:T(2,128)}) custom-call(bf16[3,256,128]{2,1,0:T(8,128)(2,1)S(1)} %get-tuple-element.118.done_ref, bf16[1024,128]{1,0:T(8,128)(2,1)S(1)} %get-tuple-element.119.rest_ref, f32[256,128]{1,0:T(8,128)S(1)} %get-tuple-element.68.tcol, ...), custom_call_target="tpu_custom_call" | custom-call | tf_op jit(solution)/shard_map/last_step/pallas_call | solution.py:570
Async XLA Ops:
  0.6 82.3 %copy-start = (bf16[256,1024]{1,0:T(8,128)(2,1)S(1)}, bf16[256,1024]{1,0:T(8,128)(2,1)}, u32[]{:S(2)}) copy-start(bf16[256,1024]{1,0:T(8,128)(2,1)} %w_hbm.1) | copy-start | bytes 1572868
  0.6 82.3 %copy-start.1 = (bf16[256,256]{1,0:T(8,128)(2,1)S(1)}, bf16[256,256]{1,0:T(8,128)(2,1)}, u32[]{:S(2)}) copy-start(bf16[256,256]{1,0:T(8,128)(2,1)} %og_hbm.1) | copy-start | bytes 393220
  0.7 82.3 %copy-start.2 = (bf16[256,256]{1,0:T(8,128)(2,1)S(1)}, bf16[256,256]{1,0:T(8,128)(2,1)}, u32[]{:S(2)}) copy-start(bf16[256,256]{1,0:T(8,128)(2,1)} %q_hbm.1) | copy-start | bytes 393220
  0.7 82.3 %copy-start.3 = (bf16[256,256]{1,0:T(8,128)(2,1)S(1)}, bf16[256,256]{1,0:T(8,128)(2,1)}, u32[]{:S(2)}) copy-start(bf16[256,256]{1,0:T(8,128)(2,1)} %k_hbm.1) | copy-start | bytes 393220
  0.7 82.3 %copy-start.4 = (bf16[256,256]{1,0:T(8,128)(2,1)S(1)}, bf16[256,256]{1,0:T(8,128)(2,1)}, u32[]{:S(2)}) copy-start(bf16[256,256]{1,0:T(8,128)(2,1)} %v_hbm.1) | copy-start | bytes 393220
  82.2 0.8 copy-start.6

commit v6 on v5

--- a/solution.py
+++ b/solution.py
@@ -22,7 +22,7 @@
 HEAD0 = CAP - CAP_HEAD
 HALF = 24
 BACK = CAP + HALF
-PARTS = ((0, 48), (48, 48), (96, 64))
+PARTS = ((0, 32), (32, 32), (64, 16), (80, 48), (128, 32))
 ROWS = 160
 
 
@@ -182,7 +182,7 @@
         goals = jnp.concatenate(goals, axis=1).astype(jnp.int32)
         rows = jnp.concatenate(rows, axis=0)
         for i in range(4):
-            pick = onehot(iota((4 * n, 1024), 0) + i * 4 * n == goals)
+            pick = onehot(iota((4 * n, goals.shape[1]), 0) + i * 4 * n == goals)
             zs[i * 4 : i * 4 + 4, at : at + n, :] = nn(pick, rows).astype(BF).reshape(4, n, 128)
 
     pl.semaphore_wait(barrier, NY - 1 + NZ - 1 + NXC - 1)
@@ -226,7 +226,7 @@
     loads[1].wait()
     loads[2].wait()
     qk = [beside(q_ref, k_ref, p) for p in range(2)]
-    pack(0, [(0, qk[0], 0, CAP, 0), (1, qk[1], 0, 8, CAP)])
+    pack(0, [(0, qk[0], 0, 32, 0)])
     send_z(zs, zr, rows_of[0], 2)
     for load in loads[3:]:
         load.wait()
@@ -238,10 +238,14 @@
         grad += nt(piece, w_ref[:, pl.ds(pl.multiple_of(y * 256, 256), 256)])
     d_out = grad.astype(BF)
     vg = [beside(v_ref, d_out, p) for p in range(2)]
-    pack(1, [(0, vg[0], 0, CAP, 0), (1, qk[1], 8, 16, CAP - 8)])
+    pack(1, [(0, vg[0], 0, 24, 0), (0, qk[0], 32, CAP, -8)])
     send_z(zs, zr, rows_of[1], 3)
-    pack(2, [(1, qk[1], 16, CAP, -16), (1, vg[1], 0, CAP, CAP - 16)])
+    pack(2, [(0, vg[0], 24, CAP, -24)])
     send_z(zs, zr, rows_of[2], 4)
+    pack(3, [(1, qk[1], 0, 24, 0), (1, vg[1], 0, 24, 24)])
+    send_z(zs, zr, rows_of[3], 20)
+    pack(4, [(1, qk[1], 24, CAP, -24), (1, vg[1], 24, CAP, -8)])
+    send_z(zs, zr, rows_of[4], 21)
 
     settle(meta_r, NZ - 1, 1, sem_r)
     r_i, l_i = iota((128, 128), 0), iota((128, 128), 1)
@@ -265,12 +269,11 @@
         fits = taken & (t < CAP_HEAD)
         t = jnp.where(l16 < 64, t, CAP - 1 - t)
         if p == 0:
-            there, empty = jnp.where(first_kind, t, t + 48), 96.0
+            there = jnp.where(first_kind, jnp.where(t < 32, t, t + 24), jnp.where(t < 24, t + 32, t + 40))
         else:
-            there = jnp.where(first_kind, jnp.where(t < 8, t + 40, t + 80), t + 120)
-            empty = float(ROWS)
+            there = t + jnp.where(first_kind, 80.0, 104.0) + jnp.where(t < 24, 0.0, jnp.where(first_kind, 24.0, 16.0))
         there = jnp.where(fits, there, -1.0)
-        tslot[p] = jnp.where(taken, there, jnp.where(first_kind, empty, -1.0))
+        tslot[p] = jnp.where(taken, there, jnp.where(first_kind, float(ROWS), -1.0))
         lower = jnp.where(t < HALF, t + CAP, -1.0)
         upper = jnp.where(t >= HALF, t + CAP - HALF, -1.0)
         tslot[2 + p] = jnp.where(fits, jnp.where(first_kind, t, lower), -1.0)
@@ -297,13 +300,14 @@
     mark = jnp.where((iota((16, 128), 0) == 0) & (iota((16, 128), 1) == 0), EMPTY, 0.0)
     mark = mark.astype(BF)
 
-    def expand(p):
-        n = (96, ROWS)[p]
-        at = iota((n + 16, 128), 0)
+    def expand(p, h):
+        first, n = ((0, 64), (0, 80), (80, 48), (80, 80))[2 * p + h]
+        at = iota((n + 16, 64), 0)
+        at = jnp.where(at < n, at + first, at - n + ROWS)
         for s in range(NZ):
-            pick = onehot(at == tslot[p, s : s + 1, :].astype(jnp.int32))
-            rows = tn(pick, jnp.concatenate([zr[s, 0:n, :], mark], axis=0))
-            xs[p, :, :, s * 8 : s * 8 + 8, :] = rows.reshape(2, 8, 8, 128).astype(BF)
+            pick = onehot(at == tslot[p, s : s + 1, h * 64 : h * 64 + 64].astype(jnp.int32))
+            rows = tn(pick, jnp.concatenate([zr[s, first : first + n, :], mark], axis=0))
+            xs[p, h, :, s * 8 : s * 8 + 8, :] = rows.reshape(8, 8, 128).astype(BF)
 
     def work(p, h):
         for i in range(4):
@@ -337,20 +341,21 @@
 
     head0, rest = pl.ds(0, HEAD0), pl.ds(HEAD0, BACK - HEAD0)
 
-    def forward(p):
-        expand(p)
-        for h in range(2):
-            send_x(xs, xr, p, h, 5 + 2 * p + h)
+    def forward(p, h):
+        expand(p, h)
+        send_x(xs, xr, p, h, 5 + 2 * p + h)
 
     def middle(p, h):
         wait_x(xs, xr, p, h, 5 + 2 * p + h)
         work(p, h)
         send_x(xbs, xbr, p, h, 9 + 2 * p + h)
 
-    def send_back(p):
+    def back_head0(p):
         wait_x(xbs, xbr, p, 0, 9 + 2 * p)
         compact_head0(p)
         send_z(zbs.at[p], zbr.at[p], head0, 14 + 2 * p)
+
+    def back_rest(p):
         wait_x(xbs, xbr, p, 1, 10 + 2 * p)
         compact_rest(p)
         send_z(zbs.at[p], zbr.at[p], rest, 15 + 2 * p)
@@ -361,7 +366,9 @@
 
     wait_z(zs, zr, rows_of[0], 2)
     wait_z(zs, zr, rows_of[1], 3)
-    forward(0)
+    forward(0, 0)
+    wait_z(zs, zr, rows_of[2], 4)
+    forward(0, 1)
     settle(full_xr, NXC - 1, 13, sem_r)
     full = jnp.max(full_xr[...], axis=0)
     full_ys[...] = full
@@ -369,13 +376,17 @@
         remote(full_ys, full_yr.at[hd], 18, ypeer(i))
     middle(0, 0)
     middle(0, 1)
-    wait_z(zs, zr, rows_of[2], 4)
-    forward(1)
-    send_back(0)
+    wait_z(zs, zr, rows_of[3], 20)
+    forward(1, 0)
+    back_head0(0)
+    wait_z(zs, zr, rows_of[4], 21)
+    forward(1, 1)
+    back_rest(0)
     middle(1, 0)
     middle(1, 1)
     remote(sum_s, sum_r, 19, zpeer(NZ // 2)[1])
-    send_back(1)
+    back_head0(1)
+    back_rest(1)
     pltpu.make_async_copy(sum_r, sum_r, sem_r.at[19]).wait()
     for p in range(2):
         cols = slice(p * HD, (p + 1) * HD)
@@ -400,8 +411,8 @@
     for i in range(1, NXC):
         pltpu.make_async_copy(full_xs, full_xs, sem_s.at[13]).wait()
     pltpu.make_async_copy(sum_s, sum_s, sem_s.at[19]).wait()
-    for i in range(3):
-        settle(zs, NZ - 1, 2 + i, sem_s, rows_of[i])
+    for rows, sem in zip(rows_of, (2, 3, 4, 20, 21)):
+        settle(zs, NZ - 1, sem, sem_s, rows)
     for p in range(2):
         for h in range(2):
             settle(xs.at[p, h], NXC - 1, 5 + 2 * p + h, sem_s)
@@ -458,9 +469,9 @@
             buf(NXC, 8, 128, dtype=F32),
             buf(8, 128, dtype=F32),
             buf(NY, 8, 128, dtype=F32),
-            pltpu.SemaphoreType.DMA((20,)),
-            pltpu.SemaphoreType.DMA((20,)),
-            pltpu.SemaphoreType.DMA((20,)),
+            pltpu.SemaphoreType.DMA((22,)),
+            pltpu.SemaphoreType.DMA((22,)),
+            pltpu.SemaphoreType.DMA((22,)),
             pltpu.SemaphoreType.DMA((6,)),
         ],
         compiler_params=pltpu.CompilerParams(
@@ -591,7 +602,7 @@
 
 def shards(*args):
     *parts, full = two_hop(*args)
-    parts = lax.cond(full[0, 0] > 0, lambda: as_parts(*padded(*args)), lambda: tuple(parts))
+    parts = lax.switch(full[0, 0], [lambda: tuple(parts), lambda: as_parts(*padded(*args))])
     return tuple(last_step(*parts))
 
 

time: 85.3 us -> 83.8 us (0.982)
  Pallas kernels: 83.4 us -> 82.2 us
    pallas_call x1, Pallas kernels: 81.5 us -> 80.3 us  [two_hop(): pl.pallas_call(kernel, name='two_hop', out_shape=(jax.ShapeDtypeStruct((3...]
where the time goes in v6:
time: 83.8 us; the launch traced here: 83.6 us
  Pallas kernels  82.2 us (98%)
  between operations  1.45 us (2%)
    pallas_call x1, Pallas kernels, two_hop(): pl.pallas_call(kernel, name='two_hop', out_shape=(jax.ShapeDtypeStruct((3...  80.3 us
    pallas_call x1, Pallas kernels, last_step(): pl.pallas_call(last_kernel, name='last_step', out_shape=(grad, grad, grad...  1.88 us

profile of v6, /device:TPU:1, one launch (start us, length us, event | category | flops | bytes accessed | tf_op | source)
XLA Modules:
  0.0 83.6 jit_solution(12669781631460890811)
XLA Ops:
  0.6 0.0 copy-start
  0.6 0.0 copy-start.1
  0.7 0.0 copy-start.2
  0.7 0.0 copy-start.3
  0.7 0.0 copy-start.4
  0.7 80.3 %two_hop.1 = (bf16[3,256,128]{2,1,0:T(8,128)(2,1)S(1)}, bf16[1024,128]{1,0:T(8,128)(2,1)S(1)}, f32[256,128]{1,0:T(8,128)S(1)}, f32[2,256]{1,0:T(2,128)S(1)}, s32[1,1]{1,0:T(1,128)}) custom-call(bf16[256,256]{1,0:T(8,128)(2,1)} %q_hbm.1, bf16[256,256]{1,0:T(8,128)(2,1)} %k_hbm.1, bf16[256,256]{1,0:T(8,128)(2,1)} %v_hbm.1, bf16[256,256]{1,0:T(8,128)(2,1)} %og_hbm.1, ...), custom_call_target="tpu_custom_call" | custom-call | tf_op jit(solution)/shard_map/two_hop/pallas_call | solution.py:432
  81.0 0.0 copy-start.6
  81.7 0.0 copy-done
  81.7 0.0 copy-done.1
  81.7 0.0 copy-done.2
  81.7 0.0 copy-done.3
  81.7 0.0 copy-done.4
  81.7 0.0 copy-done.6
  81.8 1.9 %last_step.1 = (bf16[256,256]{1,0:T(8,128)(2,1)}, bf16[256,256]{1,0:T(8,128)(2,1)}, bf16[256,256]{1,0:T(8,128)(2,1)}, f32[2,256]{1,0:T(2,128)}) custom-call(bf16[3,256,128]{2,1,0:T(8,128)(2,1)S(1)} %get-tuple-element.118.done_ref, bf16[1024,128]{1,0:T(8,128)(2,1)S(1)} %get-tuple-element.119.rest_ref, f32[256,128]{1,0:T(8,128)S(1)} %get-tuple-element.68.tcol, ...), custom_call_target="tpu_custom_call" | custom-call | tf_op jit(solution)/shard_map/last_step/pallas_call | solution.py:581
  (1 shorter events, 0.0 us)
Async XLA Ops:
  0.6 81.1 %copy-start = (bf16[256,1024]{1,0:T(8,128)(2,1)S(1)}, bf16[256,1024]{1,0:T(8,128)(2,1)}, u32[]{:S(2)}) copy-start(bf16[256,1024]{1,0:T(8,128)(2,1)} %w_hbm.1) | copy-start | bytes 1572868
  0.6 81.1 %copy-start.1 = (bf16[256,256]{1,0:T(8,128)(2,1)S(1)}, bf16[256,256]{1,0:T(8,128)(2,1)}, u32[]{:S(2)}) copy-start(bf16[256,256]{1,0:T(8,128)(2,1)} %og_hbm.1) | copy-start | bytes 393220
  0.7 81.1 %copy-start.2 = (bf16[256,256]{1,0:T(8,128)(2,1)S(1)}, bf16[256,256]{1,0:T(8,128)(2,1)}, u32[]{:S(2)}) copy-start(bf16[256,256]{1,0:T(8,128)(2,1)} %q_hbm.1) | copy-start | bytes 393220
  0.7 81.1 %copy-start.3 = (bf16[256,256]{1,0:T(8,128)(2,1)S(1)}, bf16[256,256]{1,0:T(8,128)(2,1)}, u32[]{:S(2)}) copy-start(bf16[256,256]{1,0:T(8,128)(2,1)} %k_hbm.1) | copy-start | bytes 393220
  0.7 81.1 %copy-start.4 = (bf16[256,256]{1,0:T(8,128)(2,1)S(1)}, bf16[256,256]{1,0:T(8,128)(2,1)}, u32[]{:S(2)}) copy-start(bf16[256,256]{1,0:T(8,128)(2,1)} %v_hbm.1) | copy-start | bytes 393220
  81.0 0.8 copy-start.6

commit v7 on v6

--- a/solution.py
+++ b/solution.py
@@ -22,7 +22,8 @@
 HEAD0 = CAP - CAP_HEAD
 HALF = 24
 BACK = CAP + HALF
-PARTS = ((0, 32), (32, 32), (64, 16), (80, 48), (128, 32))
+PARTS = ((0, 32), (32, 16), (48, 32), (80, 16), (96, 32), (128, 32))
+NEEDS = (((0, 80),), ((0, 96),), ((32, 16), (96, 32)), ((96, 64),))
 ROWS = 160
 
 
@@ -134,17 +135,14 @@
     earlier = onehot(sub < lane)
     ones = jnp.ones((256, 256), BF)
     before = onehot((sub // 16 == lane // 16) & (lane < sub))
-    member, count, zof = [], [], []
-    for h in range(4):
+    member, count, zof, poses, targets = [], [], [], [], []
+
+    def place_rows(h):
         ids = ids_ref[h]
         row = ((ids >> 2) & 15) * 16 + (ids >> 6) * 4 + (ids & 3)
         zof.append((((row >> 4) + (h % 2) * (NZ // 2)) & (NZ - 1)).astype(F32))
         member.append(onehot(sub == row))
         count.append(nn(member[h], ones).astype(BF))
-    poses, targets = [], []
-    meta = jnp.zeros((8, 128), F32)
-    mrow = iota((8, 128), 0)
-    for h in range(4):
         place = nn(before, count[h]) + nn(member[h], earlier)
         nth = jnp.sum(member[h].astype(F32) * place, axis=0, keepdims=True)
         fits = nth < CAP_HEAD
@@ -154,12 +152,6 @@
         targets.append(jnp.where(fits, back, -1.0))
         targets.append(jnp.where(fits & (pos < HALF), back + CAP, -1.0))
         targets.append(jnp.where(fits & (pos >= HALF), back + CAP - HALF, -1.0))
-        held = nt(jnp.ones((8, 256), BF), member[h])
-        meta = jnp.where(mrow == 2 * h, held[:, :128], meta)
-        meta = jnp.where(mrow == 2 * h + 1, held[:, 128:], meta)
-    meta_s[...] = meta.astype(BF)
-    meta_r[pl.ds(z, 1)] = meta.astype(BF)[None]
-    tcol[...] = jnp.concatenate(targets + [jnp.zeros((128 - 12, 256), F32)], axis=0).T
 
     def beside(a_ref, b, p):
         a = a_ref[:, p * 128 : (p + 1) * 128].astype(F32)
@@ -185,6 +177,13 @@
             pick = onehot(iota((4 * n, goals.shape[1]), 0) + i * 4 * n == goals)
             zs[i * 4 : i * 4 + 4, at : at + n, :] = nn(pick, rows).astype(BF).reshape(4, n, 128)
 
+    for h in range(2):
+        place_rows(h)
+    loads[1].wait()
+    loads[2].wait()
+    qk = [beside(q_ref, k_ref, 0)]
+    pack(0, [(0, qk[0], 0, 32, 0)])
+
     pl.semaphore_wait(barrier, NY - 1 + NZ - 1 + NXC - 1)
 
     def remote(src, dst, sem, peer):
@@ -199,9 +198,6 @@
 
     for i in range(1, NY):
         remote(og_hbm, ogr.at[hd], 0, ypeer(i))
-    for i in zorder:
-        remote(meta_s, meta_r.at[z], 1, zpeer(i)[1])
-
     def send_z(src, dst, rows, sem):
         for i in zorder:
             to, peer = zpeer(i)
@@ -223,29 +219,42 @@
         pltpu.make_async_copy(src.at[p, i, xc], dst.at[p, i, xc], sem_l.at[sem]).wait()
 
     rows_of = [pl.ds(at, n) for at, n in PARTS]
-    loads[1].wait()
-    loads[2].wait()
-    qk = [beside(q_ref, k_ref, p) for p in range(2)]
-    pack(0, [(0, qk[0], 0, 32, 0)])
     send_z(zs, zr, rows_of[0], 2)
+    for h in range(2, 4):
+        place_rows(h)
+    qk.append(beside(q_ref, k_ref, 1))
+    pack(1, [(1, qk[1], 0, 16, 0)])
+    send_z(zs, zr, rows_of[1], 3)
+    meta = jnp.zeros((8, 128), F32)
+    mrow = iota((8, 128), 0)
+    for h in range(4):
+        held = nt(jnp.ones((8, 256), BF), member[h])
+        meta = jnp.where(mrow == 2 * h, held[:, :128], meta)
+        meta = jnp.where(mrow == 2 * h + 1, held[:, 128:], meta)
+    meta_s[...] = meta.astype(BF)
+    meta_r[pl.ds(z, 1)] = meta.astype(BF)[None]
+    for i in zorder:
+        remote(meta_s, meta_r.at[z], 1, zpeer(i)[1])
+    tcol[...] = jnp.concatenate(targets + [jnp.zeros((128 - 12, 256), F32)], axis=0).T
     for load in loads[3:]:
         load.wait()
-    settle(ogr, NY - 1, 0, sem_r)
     grad = jnp.zeros((256, 256), F32)
     for i in range(NY):
         y = (hd + i) % NY
+        if i == 1:
+            settle(ogr, NY - 1, 0, sem_r)
         piece = og_ref[...] if i == 0 else ogr[pl.ds(y, 1)][0]
         grad += nt(piece, w_ref[:, pl.ds(pl.multiple_of(y * 256, 256), 256)])
     d_out = grad.astype(BF)
     vg = [beside(v_ref, d_out, p) for p in range(2)]
-    pack(1, [(0, vg[0], 0, 24, 0), (0, qk[0], 32, CAP, -8)])
-    send_z(zs, zr, rows_of[1], 3)
-    pack(2, [(0, vg[0], 24, CAP, -24)])
+    pack(2, [(0, vg[0], 0, 24, 0), (0, qk[0], 32, CAP, -8)])
     send_z(zs, zr, rows_of[2], 4)
-    pack(3, [(1, qk[1], 0, 24, 0), (1, vg[1], 0, 24, 24)])
+    pack(3, [(0, vg[0], 24, CAP, -24)])
     send_z(zs, zr, rows_of[3], 20)
-    pack(4, [(1, qk[1], 24, CAP, -24), (1, vg[1], 24, CAP, -8)])
+    pack(4, [(1, vg[1], 0, 24, 0), (1, qk[1], 16, 24, 8)])
     send_z(zs, zr, rows_of[4], 21)
+    pack(5, [(1, qk[1], 24, CAP, -24), (1, vg[1], 24, CAP, -8)])
+    send_z(zs, zr, rows_of[5], 22)
 
     settle(meta_r, NZ - 1, 1, sem_r)
     r_i, l_i = iota((128, 128), 0), iota((128, 128), 1)
@@ -269,9 +278,9 @@
         fits = taken & (t < CAP_HEAD)
         t = jnp.where(l16 < 64, t, CAP - 1 - t)
         if p == 0:
-            there = jnp.where(first_kind, jnp.where(t < 32, t, t + 24), jnp.where(t < 24, t + 32, t + 40))
+            there = jnp.where(first_kind, jnp.where(t < 32, t, t + 40), jnp.where(t < 24, t + 48, t + 56))
         else:
-            there = t + jnp.where(first_kind, 80.0, 104.0) + jnp.where(t < 24, 0.0, jnp.where(first_kind, 24.0, 16.0))
+            there = jnp.where(first_kind, jnp.where(t < 16, t + 32, t + 104), jnp.where(t < 24, t + 96, t + 120))
         there = jnp.where(fits, there, -1.0)
         tslot[p] = jnp.where(taken, there, jnp.where(first_kind, float(ROWS), -1.0))
         lower = jnp.where(t < HALF, t + CAP, -1.0)
@@ -301,12 +310,16 @@
     mark = mark.astype(BF)
 
     def expand(p, h):
-        first, n = ((0, 64), (0, 80), (80, 48), (80, 80))[2 * p + h]
-        at = iota((n + 16, 64), 0)
-        at = jnp.where(at < n, at + first, at - n + ROWS)
+        needs = NEEDS[2 * p + h]
+        i = iota((sum(n for _, n in needs) + 16, 64), 0)
+        at, done = i - i.shape[0] + 16 + ROWS, i.shape[0] - 16
+        for first, n in reversed(needs):
+            done -= n
+            at = jnp.where(i < done + n, i - done + first, at)
         for s in range(NZ):
             pick = onehot(at == tslot[p, s : s + 1, h * 64 : h * 64 + 64].astype(jnp.int32))
-            rows = tn(pick, jnp.concatenate([zr[s, first : first + n, :], mark], axis=0))
+            rows = [zr[s, first : first + n, :] for first, n in needs]
+            rows = tn(pick, jnp.concatenate(rows + [mark], axis=0))
             xs[p, h, :, s * 8 : s * 8 + 8, :] = rows.reshape(8, 8, 128).astype(BF)
 
     def work(p, h):
@@ -366,8 +379,9 @@
 
     wait_z(zs, zr, rows_of[0], 2)
     wait_z(zs, zr, rows_of[1], 3)
+    wait_z(zs, zr, rows_of[2], 4)
     forward(0, 0)
-    wait_z(zs, zr, rows_of[2], 4)
+    wait_z(zs, zr, rows_of[3], 20)
     forward(0, 1)
     settle(full_xr, NXC - 1, 13, sem_r)
     full = jnp.max(full_xr[...], axis=0)
@@ -376,10 +390,10 @@
         remote(full_ys, full_yr.at[hd], 18, ypeer(i))
     middle(0, 0)
     middle(0, 1)
-    wait_z(zs, zr, rows_of[3], 20)
+    wait_z(zs, zr, rows_of[4], 21)
     forward(1, 0)
     back_head0(0)
-    wait_z(zs, zr, rows_of[4], 21)
+    wait_z(zs, zr, rows_of[5], 22)
     forward(1, 1)
     back_rest(0)
     middle(1, 0)
@@ -411,7 +425,7 @@
     for i in range(1, NXC):
         pltpu.make_async_copy(full_xs, full_xs, sem_s.at[13]).wait()
     pltpu.make_async_copy(sum_s, sum_s, sem_s.at[19]).wait()
-    for rows, sem in zip(rows_of, (2, 3, 4, 20, 21)):
+    for rows, sem in zip(rows_of, (2, 3, 4, 20, 21, 22)):
         settle(zs, NZ - 1, sem, sem_s, rows)
     for p in range(2):
         for h in range(2):
@@ -469,9 +483,9 @@
             buf(NXC, 8, 128, dtype=F32),
             buf(8, 128, dtype=F32),
             buf(NY, 8, 128, dtype=F32),
-            pltpu.SemaphoreType.DMA((22,)),
-            pltpu.SemaphoreType.DMA((22,)),
-            pltpu.SemaphoreType.DMA((22,)),
+            pltpu.SemaphoreType.DMA((23,)),
+            pltpu.SemaphoreType.DMA((23,)),
+            pltpu.SemaphoreType.DMA((23,)),
             pltpu.SemaphoreType.DMA((6,)),
         ],
         compiler_params=pltpu.CompilerParams(

time: 83.8 us -> 83.3 us (level)
  no operation moved by 1% of the time
where the time goes in v7:
time: 83.3 us; the launch traced here: 83.2 us
  Pallas kernels  81.7 us (98%)
  between operations  1.45 us (2%)
    pallas_call x1, Pallas kernels, two_hop(): pl.pallas_call(kernel, name='two_hop', out_shape=(jax.ShapeDtypeStruct((3...  79.8 us
    pallas_call x1, Pallas kernels, last_step(): pl.pallas_call(last_kernel, name='last_step', out_shape=(grad, grad, grad...  1.88 us

profile of v7, /device:TPU:1, one launch (start us, length us, event | category | flops | bytes accessed | tf_op | source)
XLA Modules:
  0.0 83.2 jit_solution(1298952347782297085)
XLA Ops:
  0.6 0.0 copy-start
  0.6 0.0 copy-start.1
  0.7 0.0 copy-start.2
  0.7 0.0 copy-start.3
  0.7 0.0 copy-start.4
  0.7 79.8 %two_hop.1 = (bf16[3,256,128]{2,1,0:T(8,128)(2,1)S(1)}, bf16[1024,128]{1,0:T(8,128)(2,1)S(1)}, f32[256,128]{1,0:T(8,128)S(1)}, f32[2,256]{1,0:T(2,128)S(1)}, s32[1,1]{1,0:T(1,128)}) custom-call(bf16[256,256]{1,0:T(8,128)(2,1)} %q_hbm.1, bf16[256,256]{1,0:T(8,128)(2,1)} %k_hbm.1, bf16[256,256]{1,0:T(8,128)(2,1)} %v_hbm.1, bf16[256,256]{1,0:T(8,128)(2,1)} %og_hbm.1, ...), custom_call_target="tpu_custom_call" | custom-call | tf_op jit(solution)/shard_map/two_hop/pallas_call | solution.py:446
  80.5 0.0 copy-start.6
  81.2 0.0 copy-done
  81.2 0.0 copy-done.1
  81.2 0.0 copy-done.2
  81.2 0.0 copy-done.3
  81.3 0.0 copy-done.4
  81.3 0.0 copy-done.6
  81.3 1.9 %last_step.1 = (bf16[256,256]{1,0:T(8,128)(2,1)}, bf16[256,256]{1,0:T(8,128)(2,1)}, bf16[256,256]{1,0:T(8,128)(2,1)}, f32[2,256]{1,0:T(2,128)}) custom-call(bf16[3,256,128]{2,1,0:T(8,128)(2,1)S(1)} %get-tuple-element.118.done_ref, bf16[1024,128]{1,0:T(8,128)(2,1)S(1)} %get-tuple-element.119.rest_ref, f32[256,128]{1,0:T(8,128)S(1)} %get-tuple-element.68.tcol, ...), custom_call_target="tpu_custom_call" | custom-call | tf_op jit(solution)/shard_map/last_step/pallas_call | solution.py:595
  (1 shorter events, 0.0 us)
Async XLA Ops:
  0.6 80.6 %copy-start = (bf16[256,1024]{1,0:T(8,128)(2,1)S(1)}, bf16[256,1024]{1,0:T(8,128)(2,1)}, u32[]{:S(2)}) copy-start(bf16[256,1024]{1,0:T(8,128)(2,1)} %w_hbm.1) | copy-start | bytes 1572868
  0.6 80.6 %copy-start.1 = (bf16[256,256]{1,0:T(8,128)(2,1)S(1)}, bf16[256,256]{1,0:T(8,128)(2,1)}, u32[]{:S(2)}) copy-start(bf16[256,256]{1,0:T(8,128)(2,1)} %og_hbm.1) | copy-start | bytes 393220
  0.7 80.6 %copy-start.2 = (bf16[256,256]{1,0:T(8,128)(2,1)S(1)}, bf16[256,256]{1,0:T(8,128)(2,1)}, u32[]{:S(2)}) copy-start(bf16[256,256]{1,0:T(8,128)(2,1)} %q_hbm.1) | copy-start | bytes 393220
  0.7 80.6 %copy-start.3 = (bf16[256,256]{1,0:T(8,128)(2,1)S(1)}, bf16[256,256]{1,0:T(8,128)(2,1)}, u32[]{:S(2)}) copy-start(bf16[256,256]{1,0:T(8,128)(2,1)} %k_hbm.1) | copy-start | bytes 393220
  0.7 80.6 %copy-start.4 = (bf16[256,256]{1,0:T(8,128)(2,1)S(1)}, bf16[256,256]{1,0:T(8,128)(2,1)}, u32[]{:S(2)}) copy-start(bf16[256,256]{1,0:T(8,128)(2,1)} %v_hbm.1) | copy-start | bytes 393220
  80.5 0.8 copy-start.6

commit v8 on v7

--- a/solution.py
+++ b/solution.py
@@ -69,23 +69,23 @@
     return jnp.where(low, dk, dq).astype(BF), jnp.where(low, swap_halves(dv), dv).astype(BF)
 
 
-def unpack(p, rows, tcol):
+def unpack(p, rows, v_rows, tcol):
     keys, values, queries = [], [], []
-    at = iota((256, NZ * BACK), 1)
+    at, v_at = iota((256, NZ * CAP), 1), iota((256, NZ * HALF), 1)
     for h in (2 * p, 2 * p + 1):
         cols = tcol[:, 3 * h : 3 * h + 3].astype(jnp.int32)
         got = nn(onehot(at == cols[:, 0:1]), rows)
-        first = nn(onehot(at == cols[:, 1:2]), rows)
-        second = nn(onehot(at == cols[:, 2:3]), rows)
+        first = nn(onehot(v_at == cols[:, 1:2]), v_rows)
+        second = nn(onehot(v_at == cols[:, 2:3]), v_rows)
         keys.append(got[:, :HD])
         queries.append(got[:, HD:])
         values.append(first[:, :HD] + second[:, HD:])
     return [jnp.concatenate(x, axis=1).astype(BF) for x in (queries, keys, values)]
 
 
-def last_kernel(done_ref, rest_ref, tcol, cs_in, dq_ref, dk_ref, dv_ref, cs_ref):
+def last_kernel(done_ref, rest_ref, rest_v_ref, tcol, cs_in, dq_ref, dk_ref, dv_ref, cs_ref):
     cs_ref[...] = cs_in[...]
-    parts = unpack(1, rest_ref[...], tcol)
+    parts = unpack(1, rest_ref[...], rest_v_ref[...], tcol)
     for i, ref in enumerate((dq_ref, dk_ref, dv_ref)):
         ref[:, 0:128] = done_ref[i]
         ref[:, 128:256] = parts[i]
@@ -93,7 +93,7 @@
 
 def kernel(
     q_hbm, k_hbm, v_hbm, og_hbm, w_hbm, ids_hbm,
-    done_ref, rest_ref, tcol, cs_ref, full_ref,
+    done_ref, rest_ref, rest_v_ref, tcol, cs_ref, full_ref,
     q_ref, k_ref, v_ref, og_ref, w_ref, ids_ref, ogr, meta_s, meta_r, zs, zr, xs, xr, yb, zb, xbs, xbr, zbs, zbr, tslot,
     sum_own, sum_s, sum_r, full_xs, full_xr, full_ys, full_yr,
     sem_s, sem_r, sem_l, sem_in,
@@ -148,10 +148,10 @@
         fits = nth < CAP_HEAD
         pos = nth if h % 2 == 0 else CAP - 1 - nth
         poses.append(jnp.where(fits, pos, -1.0))
-        back = zof[h] * BACK + pos
-        targets.append(jnp.where(fits, back, -1.0))
-        targets.append(jnp.where(fits & (pos < HALF), back + CAP, -1.0))
-        targets.append(jnp.where(fits & (pos >= HALF), back + CAP - HALF, -1.0))
+        targets.append(jnp.where(fits, zof[h] * CAP + pos, -1.0))
+        back = zof[h] * HALF + pos
+        targets.append(jnp.where(fits & (pos < HALF), back, -1.0))
+        targets.append(jnp.where(fits & (pos >= HALF), back - HALF, -1.0))
 
     def beside(a_ref, b, p):
         a = a_ref[:, p * 128 : (p + 1) * 128].astype(F32)
@@ -411,11 +411,17 @@
     for i in range(1, NY):
         full = jnp.maximum(full, full_yr[pl.ds((hd + i) % NY, 1)][0])
     full_ref[0, 0] = jnp.max(full).astype(jnp.int32)
+    def gather(p):
+        for i in range(NZ):
+            rest_ref[i * CAP : i * CAP + CAP, :] = zbr[p, i, 0:CAP, :]
+            rest_v_ref[i * HALF : i * HALF + HALF, :] = zbr[p, i, CAP:BACK, :]
+
     wait_back(0)
-    for i, part in enumerate(unpack(0, zbr[0].reshape(NZ * BACK, 128), tcol)):
+    gather(0)
+    for i, part in enumerate(unpack(0, rest_ref[...], rest_v_ref[...], tcol)):
         done_ref[i] = part
     wait_back(1)
-    rest_ref[...] = zbr[1].reshape(NZ * BACK, 128)
+    gather(1)
 
     for i in range(1, NY):
         pltpu.make_async_copy(og_ref, og_ref, sem_s.at[0]).wait()
@@ -448,13 +454,14 @@
         name="two_hop",
         out_shape=(
             jax.ShapeDtypeStruct((3, frames, width // 2), BF),
-            jax.ShapeDtypeStruct((NZ * BACK, 128), BF),
+            jax.ShapeDtypeStruct((NZ * CAP, 128), BF),
+            jax.ShapeDtypeStruct((NZ * HALF, 128), BF),
             jax.ShapeDtypeStruct((frames, 128), F32),
             jax.ShapeDtypeStruct((2, width), F32),
             jax.ShapeDtypeStruct((1, 1), jnp.int32),
         ),
         in_specs=[pl.BlockSpec(memory_space=pl.ANY)] * 6,
-        out_specs=(vmem,) * 4 + (pl.BlockSpec(memory_space=pltpu.SMEM),),
+        out_specs=(vmem,) * 5 + (pl.BlockSpec(memory_space=pltpu.SMEM),),
         scratch_shapes=[
             buf(frames, width),
             buf(frames, width),
@@ -588,7 +595,7 @@
     return (query_grad, key_grad, value_grad, centroid_sums)
 
 
-def last_step(done, rest, tcol, sums):
+def last_step(done, rest, rest_v, tcol, sums):
     frames, width = done.shape[1], 2 * done.shape[2]
     vmem = pl.BlockSpec(memory_space=pltpu.VMEM)
     grad = jax.ShapeDtypeStruct((frames, width), BF)
@@ -596,22 +603,23 @@
         last_kernel,
         name="last_step",
         out_shape=(grad, grad, grad, jax.ShapeDtypeStruct(sums.shape, F32)),
-        in_specs=[vmem] * 4,
+        in_specs=[vmem] * 5,
         out_specs=(vmem,) * 4,
         compiler_params=pltpu.CompilerParams(vmem_limit_bytes=16 << 20),
-    )(done, rest, tcol, sums)
+    )(done, rest, rest_v, tcol, sums)
 
 
 def as_parts(dq, dk, dv, sums):
     frames = dq.shape[0]
     done = jnp.stack([x[:, :128] for x in (dq, dk, dv)])
     rest = [jnp.concatenate([dk[:, at : at + HD], dq[:, at : at + HD]], axis=1) for at in (128, 192)]
-    rest = jnp.concatenate(rest + [dv[:, 128:], jnp.zeros((NZ * BACK - 3 * frames, 128), BF)])
+    rest = jnp.concatenate(rest + [jnp.zeros((NZ * CAP - 2 * frames, 128), BF)])
+    rest_v = jnp.concatenate([dv[:, 128:], jnp.zeros((NZ * HALF - frames, 128), BF)])
     at = jnp.arange(frames, dtype=F32)[:, None]
     none = jnp.full((frames, 1), -1.0, F32)
-    second = [at, at + 2 * frames, none, at + frames, none, at + 2 * frames]
+    second = [at, at, none, at + frames, none, at]
     cols = [jnp.zeros((frames, 6), F32)] + second + [jnp.zeros((frames, 116), F32)]
-    return done, rest, jnp.concatenate(cols, axis=1), sums
+    return done, rest, rest_v, jnp.concatenate(cols, axis=1), sums
 
 
 def shards(*args):

time: 83.3 us -> 82.8 us (level)
  no operation moved by 1% of the time
where the time goes in v8:
time: 82.8 us; the launch traced here: 82.6 us
  Pallas kernels  81.1 us (98%)
  between operations  1.45 us (2%)
    pallas_call x1, Pallas kernels, two_hop(): pl.pallas_call(kernel, name='two_hop', out_shape=(jax.ShapeDtypeStruct((3...  79.7 us

profile of v8, /device:TPU:1, one launch (start us, length us, event | category | flops | bytes accessed | tf_op | source)
XLA Modules:
  0.0 82.6 jit_solution(12385800021942576406)
XLA Ops:
  0.6 0.0 copy-start
  0.6 0.0 copy-start.1
  0.7 0.0 copy-start.2
  0.7 0.0 copy-start.3
  0.7 0.0 copy-start.4
  0.7 79.7 %two_hop.1 = (bf16[3,256,128]{2,1,0:T(8,128)(2,1)S(1)}, bf16[640,128]{1,0:T(8,128)(2,1)S(1)}, bf16[384,128]{1,0:T(8,128)(2,1)S(1)}, f32[256,128]{1,0:T(8,128)S(1...) custom-call(bf16[256,256]{1,0:T(8,128)(2,1)} %q_hbm.1, bf16[256,256]{1,0:T(8,128)(2,1)} %k_hbm.1, bf16[256,256]{1,0:T(8,128)(2,1)} %v_hbm.1, ...), custom_call_target="tpu_custom_call" | custom-call | tf_op jit(solution)/shard_map/two_hop/pallas_call | solution.py:452
  80.4 0.0 copy-start.6
  81.1 0.0 copy-done
  81.1 0.0 copy-done.1
  81.1 0.0 copy-done.2
  81.1 0.0 copy-done.3
  81.1 0.0 copy-done.4
  81.1 0.0 copy-done.6
  81.2 1.4 %last_step.1 = (bf16[256,256]{1,0:T(8,128)(2,1)}, bf16[256,256]{1,0:T(8,128)(2,1)}, bf16[256,256]{1,0:T(8,128)(2,1)}, f32[2,256]{1,0:T(2,128)}) custom-call(bf16[3,256,128]{2,1,0:T(8,128)(2,1)S(1)} %get-tuple-element.127.done_ref, bf16[640,128]{1,0:T(8,128)(2,1)S(1)} %get-tuple-element.128.rest_ref, bf16[384,128]{1,0:T(8,128)(2,1)S(1)} %get-tuple-element.129.rest_v_ref, ...), custom_call_target="tpu_custom_call" | custom-call | tf_op jit(solution)/shard_map/last_step/pallas_call | solution.py:602
  (1 shorter events, 0.0 us)
Async XLA Ops:
  0.6 80.5 %copy-start = (bf16[256,1024]{1,0:T(8,128)(2,1)S(1)}, bf16[256,1024]{1,0:T(8,128)(2,1)}, u32[]{:S(2)}) copy-start(bf16[256,1024]{1,0:T(8,128)(2,1)} %w_hbm.1) | copy-start | bytes 1572868
  0.6 80.5 %copy-start.1 = (bf16[256,256]{1,0:T(8,128)(2,1)S(1)}, bf16[256,256]{1,0:T(8,128)(2,1)}, u32[]{:S(2)}) copy-start(bf16[256,256]{1,0:T(8,128)(2,1)} %og_hbm.1) | copy-start | bytes 393220
  0.7 80.5 %copy-start.2 = (bf16[256,256]{1,0:T(8,128)(2,1)S(1)}, bf16[256,256]{1,0:T(8,128)(2,1)}, u32[]{:S(2)}) copy-start(bf16[256,256]{1,0:T(8,128)(2,1)} %q_hbm.1) | copy-start | bytes 393220
  0.7 80.5 %copy-start.3 = (bf16[256,256]{1,0:T(8,128)(2,1)S(1)}, bf16[256,256]{1,0:T(8,128)(2,1)}, u32[]{:S(2)}) copy-start(bf16[256,256]{1,0:T(8,128)(2,1)} %k_hbm.1) | copy-start | bytes 393220
  0.7 80.5 %copy-start.4 = (bf16[256,256]{1,0:T(8,128)(2,1)S(1)}, bf16[256,256]{1,0:T(8,128)(2,1)}, u32[]{:S(2)}) copy-start(bf16[256,256]{1,0:T(8,128)(2,1)} %v_hbm.1) | copy-start | bytes 393220
  80.4 0.8 copy-start.6
